TPU v7x, 128 devices: a whole 4x4x4 slice. The times are simulated.
128 devices in a mesh: gx: 8 (over z, y_hi), gy: 8 (over x, core), gz: 2 (over y_lo).
Axes of the slice: x: 4, y: 4 (y_hi: 2, y_lo: 2; y = y_hi * 2 + y_lo), z: 4, core: 2. Of those that a mesh axis runs over, the one named last changes fastest.
Arguments:
- positions: float32 [3, 8, 8, 2, 128], P(None, 'gx', 'gy', 'gz'), may hold values from 0 to 24, as said below
- occupancy: int32 [8, 8, 2, 128], P('gx', 'gy', 'gz'), may hold values from 0 to 1
- neighbours: int32 [56, 8, 8, 2, 128], P(None, 'gx', 'gy', 'gz'), may hold values from 0 to 639, as said below
- keep: int32 [56, 8, 8, 2, 128], P(None, 'gx', 'gy', 'gz'), may hold values from 0 to 1, as said below
- face_x: int32 [8, 8, 2, 2, 64], P('gx', 'gy', 'gz'), may hold values from 0 to 127, as said below
- face_y: int32 [8, 8, 2, 2, 128], P('gx', 'gy', 'gz'), may hold values from 0 to 255, as said below
- face_z: int32 [8, 8, 2, 128], P('gx', 'gy', 'gz'), may hold values from 0 to 511, as said below
- radial_one: float32 [8, 128], replicated, may hold values from -2 to 2
- mix_one: bfloat16 [384, 128], replicated, may hold values from -0.3125 to 0.3125
- embed: float32 [128], replicated, may hold values from -3 to 3
- radial_two: float32 [8, 128], replicated, may hold values from -3 to 3
- mix_two: bfloat16 [384, 128], replicated, may hold values from -0.3125 to 0.3125
- read_one: float32 [128], replicated, may hold values from -0.4375 to 0.4375
- read_hidden: float32 [128, 16], replicated, may hold values from -0.5 to 0.5
- read_out: float32 [16], replicated, may hold values from -1.5 to 1.5
Outputs:
- energies: float32 [8, 8, 2, 128], P('gx', 'gy', 'gz')
- forces: float32 [3, 8, 8, 2, 128], P(None, 'gx', 'gy', 'gz')
Inputs may be any that keep to these rules, and one draw needn't show every extreme that they name: `positions`: coordinates in angstrom in the box's own frame; any two atoms named by one list entry lie at least 1.4 apart, counted with the periodic images along gx and gy. `neighbours`: Where the neighbour would lie outside the slab, the entry names the atom at the opposite offset and keep is 0. `keep`: 0 where the atom's slot or the neighbour's slot is empty, or the entry is a pad. `face_x`: distinct own slots; entry 0 lists the slots seen by the lower box, entry 1 by the higher box. `face_y`: distinct rows of the own and x-ghost part of the list; entry 0 for the lower box along gy, entry 1 for the higher. `face_z`: distinct rows of the own, x- and y-ghost part of the list, seen by the other box along gz.
All inputs are finite; a program needn't handle non-finite values.
Results may differ from a plain program's by a relative error of at most 0.01.
Values may be sent and summed in bfloat16 or wider, within the bound.
A program may use at most 128 MiB of HBM per device.

v0:
```python
import functools
import math

import jax
import jax.numpy as jnp
from jax import lax
from jax.experimental import pallas as pl
from jax.experimental.pallas import tpu as pltpu
from jax.sharding import PartitionSpec as P

F32 = jnp.float32
BF16 = jnp.bfloat16
NB = 8
NM = 9
ATOMS = 128
NEIGH = 56
EXT = 640
C = 128
STEP_XY = 4 * 1.8
STEP_Z = 8 * 1.8
CUTOFF = 5.0
SPREAD = 0.4
HIGHEST = lax.Precision.HIGHEST
R3 = 3.0**0.5
R5 = 5.0**0.5
R15 = 15.0**0.5
MESH = pl.DeviceIdType.MESH

POS, FEAT, GRAD, FORCE = 0, 5, 10, 15
X_UP, X_DOWN, Y_UP, Y_DOWN, Z_SWAP = 0, 1, 2, 3, 4


def nn(a, b, **kw):
    return jnp.dot(a, b, preferred_element_type=F32, **kw)


def nt(a, b, **kw):
    return lax.dot_general(a, b, (((1,), (1,)), ((), ())), preferred_element_type=F32, **kw)


def tn(a, b, **kw):
    return lax.dot_general(a, b, (((0,), (0,)), ((), ())), preferred_element_type=F32, **kw)


def poly(x, coefficients):
    total = coefficients[-1]
    for c in coefficients[-2::-1]:
        total = total * x + c
    return total


COS_C = [(-1.0) ** i * math.pi ** (2 * i) / math.factorial(2 * i) for i in range(8)]
SIN_C = [(-1.0) ** i * math.pi ** (2 * i + 1) / math.factorial(2 * i + 1) for i in range(7)]


def geometry(vx, vy, vz, w, derivative):
    sq = jnp.where(w > 0.0, vx * vx + vy * vy + vz * vz, 1.0)
    inv_r = lax.rsqrt(sq)
    r = sq * inv_r
    ux, uy, uz = vx * inv_r, vy * inv_r, vz * inv_r
    s = jnp.minimum(r * (1.0 / CUTOFF), 1.0)
    t = 1.0 - s * s
    x = s - 0.5
    x2 = x * x
    sin1 = poly(x2, COS_C)
    cos1 = -x * poly(x2, SIN_C)
    p = w * ((2.0 / CUTOFF) ** 0.5 * inv_r)
    pt = p * t
    q = pt * t
    twice = 2.0 * cos1
    sins = [sin1, twice * sin1]
    for k in range(2, NB):
        sins.append(twice * sins[-1] - sins[-2])
    basis = [q * v for v in sins]
    if not derivative:
        return (ux, uy, uz), inv_r, basis, None
    coss = [cos1, twice * cos1 - 1.0]
    for k in range(2, NB):
        coss.append(twice * coss[-1] - coss[-2])
    q5 = q * (math.pi / CUTOFF)
    low = q * inv_r + pt * (s * (4.0 / CUTOFF))
    slopes = [(k + 1.0) * q5 * coss[k] - low * sins[k] for k in range(NB)]
    return (ux, uy, uz), inv_r, basis, slopes


def harmonics(ux, uy, uz):
    return [
        None,
        R3 * ux,
        R3 * uy,
        R3 * uz,
        R15 * ux * uy,
        R15 * uy * uz,
        0.5 * R5 * (3.0 * uz * uz - 1.0),
        R15 * ux * uz,
        0.5 * R15 * (ux * ux - uy * uy),
    ]


def edge_pull(gamma, unit, inv_r, basis, slopes):
    ux, uy, uz = unit
    ang = harmonics(ux, uy, uz)
    q = [gamma(0, k) for k in range(NB)]
    p = [None] * NM
    for m in range(1, NM):
        for k in range(NB):
            value = gamma(m, k)
            q[k] = q[k] + value * ang[m]
            term = value * basis[k]
            p[m] = term if k == 0 else p[m] + term
    radial = q[0] * slopes[0]
    for k in range(1, NB):
        radial = radial + q[k] * slopes[k]
    gx = R3 * p[1] + R15 * (uy * p[4] + uz * p[7] + ux * p[8])
    gy = R3 * p[2] + R15 * (ux * p[4] + uz * p[5] - uy * p[8])
    gz = R3 * p[3] + R15 * (uy * p[5] + ux * p[7]) + (3.0 * R5) * uz * p[6]
    along = radial - (gx * ux + gy * uy + gz * uz) * inv_r
    return gx * inv_r + along * ux, gy * inv_r + along * uy, gz * inv_r + along * uz


def squares(parts):
    total = parts[0] * parts[0]
    for part in parts[1:]:
        total = total + part * part
    return total


def onehot(rows, first, picks):
    ids = lax.broadcasted_iota(jnp.int32, (rows, picks.shape[1]), 0) + first
    return jnp.where(ids == picks, 1.0, 0.0).astype(BF16)


def split3(x):
    hi = x.astype(BF16)
    rest = x - hi.astype(F32)
    mid = rest.astype(BF16)
    low = (rest - mid.astype(F32)).astype(BF16)
    return hi, mid, low


def kernel(
    pos, occ, nbr, keep, fx, fy, fz, r1, mix1, emb, r2, mix2, ro1, rh, ro2,
    e_out, f_out,
    xt, xsend, xcol, key, wgt, weight, ohx, ohy, ohz,
    r1b, r2b, mixt1, mixt2, embb, amp, amp2, inv, ht, hn, hsend, hxrecv, smat, geo, ut,
    gam, dv, dh, gsend, gzr, gyr, gxr, frow, fsend, frecv, dm,
    send, recv,
):
    cx, cy, cz = lax.axis_index("gx"), lax.axis_index("gy"), lax.axis_index("gz")
    nx, ny = lax.axis_size("gx"), lax.axis_size("gy")
    peers = [
        {"gx": lax.rem(cx + 1, nx)},
        {"gx": lax.rem(cx + nx - 1, nx)},
        {"gy": lax.rem(cy + 1, ny)},
        {"gy": lax.rem(cy + ny - 1, ny)},
        {"gz": 1 - cz},
    ]

    def copy(phase, way, src, dst):
        i = phase + way
        return pltpu.make_async_remote_copy(
            src_ref=src, dst_ref=dst, send_sem=send.at[i], recv_sem=recv.at[i],
            device_id=peers[way], device_id_type=MESH,
        )

    barrier = pltpu.get_barrier_semaphore()
    for peer in peers:
        pl.semaphore_signal(barrier, inc=1, device_id=peer, device_id_type=MESH)

    xt[0] = jnp.zeros((8, ATOMS), F32)
    for d in range(3):
        xt[0, d : d + 1, :] = pos[d, 0, 0]
    pick_x = jnp.concatenate([fx[0, 0, 0, 1:2, :], fx[0, 0, 0, 0:1, :]], axis=1)
    pick_up = fy[0, 0, 0, 1:2, :]
    pick_down = fy[0, 0, 0, 0:1, :]
    pick_z = fz[0, 0]

    def lane_pick(picks, blocks):
        wide = jnp.broadcast_to(picks, (8, ATOMS))
        low = wide & (ATOMS - 1)
        total = jnp.take_along_axis(xt[0], low, axis=1)
        for b in range(1, blocks):
            total = jnp.where(wide >= b * ATOMS, jnp.take_along_axis(xt[b], low, axis=1), total)
        return total

    row = lax.broadcasted_iota(jnp.int32, (8, ATOMS), 0)
    lane = lax.broadcasted_iota(jnp.int32, (8, ATOMS), 1)

    xsend[0] = lane_pick(pick_x, 1)
    pl.semaphore_wait(barrier, 5)
    pos_up = copy(POS, X_UP, xsend.at[0], xsend.at[4])
    pos_down = copy(POS, X_DOWN, xsend.at[0], xsend.at[5])
    pos_up.start()
    pos_down.start()

    for j in range(NEIGH):
        kept = keep[j, 0, 0]
        slot = nbr[j, 0, 0]
        key[j : j + 1, :] = jnp.where(kept > 0, slot, -1)
        wgt[j : j + 1, :] = slot
    ohx[...] = onehot(ATOMS, 0, pick_x)
    ohy[:, 0:ATOMS] = onehot(2 * ATOMS, 0, pick_up)
    ohy[:, ATOMS : 2 * ATOMS] = onehot(2 * ATOMS, 0, pick_down)
    ohz[...] = onehot(4 * ATOMS, 0, pick_z)

    def weight_block(i, carry):
        base = i * 64
        rows = [lax.broadcasted_iota(jnp.int32, (8, ATOMS), 0) + base + 8 * t for t in range(8)]
        total = [jnp.zeros((8, ATOMS), F32) for t in range(8)]
        for j in range(NEIGH):
            one = jnp.broadcast_to(key[j : j + 1, :], (8, ATOMS))
            for t in range(8):
                total[t] = total[t] + jnp.where(rows[t] == one, 1.0, 0.0)
        for t in range(8):
            weight[pl.ds(pl.multiple_of(base + 8 * t, 8), 8), :] = total[t]
        return carry

    lax.fori_loop(0, 3, weight_block, 0)
    pos_up.wait()
    pos_down.wait()
    side = jnp.where(row == 0, STEP_XY, 0.0)
    xt[1] = jnp.where(lane < 64, xsend[4] - side, xsend[5] + side)
    xsend[1] = lane_pick(pick_up, 2)
    xsend[2] = lane_pick(pick_down, 2)
    pos_up = copy(POS, Y_UP, xsend.at[1], xsend.at[6])
    pos_down = copy(POS, Y_DOWN, xsend.at[2], xsend.at[7])
    pos_up.start()
    pos_down.start()
    for k in range(NB):
        r1b[k] = SPREAD * jnp.broadcast_to(r1[k : k + 1, :], (C, ATOMS)).T
        r2b[k] = SPREAD * jnp.broadcast_to(r2[k : k + 1, :], (C, ATOMS)).T
    lax.fori_loop(3, 6, weight_block, 0)
    pos_up.wait()
    pos_down.wait()
    side = jnp.where(row == 1, STEP_XY, 0.0)
    xt[2] = xsend[6] - side
    xt[3] = xsend[7] + side
    xsend[3] = lane_pick(pick_z, 4)
    pos_z = copy(POS, Z_SWAP, xsend.at[3], xsend.at[8])
    pos_z.start()
    for b in range(3):
        rows = slice(b * C, (b + 1) * C)
        mixt1[:, rows] = mix1[rows, :].astype(F32).T.astype(BF16)
        mixt2[:, rows] = mix2[rows, :].astype(F32).T.astype(BF16)
    embb[0] = jnp.broadcast_to(emb[...], (C, ATOMS)).T
    embb[1] = jnp.broadcast_to(ro1[...], (C, ATOMS)).T
    lax.fori_loop(6, 10, weight_block, 0)
    for b in range(4):
        xcol[b * ATOMS : (b + 1) * ATOMS, :] = xt[b].T
    pos_z.wait()
    upward = jnp.where(cz == 0, STEP_Z, -STEP_Z)
    xt[4] = xsend[8] + jnp.where(row == 2, upward, 0.0)
    xcol[4 * ATOMS : 5 * ATOMS, :] = xt[4].T

    slots = wgt[...]
    kept = jnp.where(key[...] >= 0, 1.0, 0.0)
    offsets = []
    for d in range(3):
        pieces = []
        for i in range(NEIGH // 8):
            wide = slots[8 * i : 8 * i + 8, :]
            low = wide & (ATOMS - 1)
            got = None
            for b in range(5):
                table = jnp.broadcast_to(xt[b, d : d + 1, :], (8, ATOMS))
                here = jnp.take_along_axis(table, low, axis=1)
                got = here if b == 0 else jnp.where(wide >= b * ATOMS, here, got)
            pieces.append(got - xt[0, d : d + 1, :])
        offsets.append(jnp.concatenate(pieces, axis=0))
    unit, _, basis, _ = geometry(*offsets, kept, False)
    ang = harmonics(*unit)
    for m in range(NM):
        total = None
        for k in range(NB):
            product = basis[k] if m == 0 else basis[k] * ang[m]
            moment = jnp.sum(product, axis=0, keepdims=True)
            term = r1b[k] * moment
            total = term if k == 0 else total + term
        amp[m] = total
    inv[0:C, :] = amp[0].astype(BF16)
    inv[C : 2 * C, :] = squares([amp[m] for m in range(1, 4)]).astype(BF16)
    inv[2 * C :, :] = squares([amp[m] for m in range(4, 9)]).astype(BF16)
    ht[0] = (nn(mixt1[...], inv[...]) + embb[0]).astype(BF16)

    hsend[0] = nn(ht[0], ohx[...]).astype(BF16)
    feat_up = copy(FEAT, X_UP, hsend.at[0], hxrecv.at[0])
    feat_down = copy(FEAT, X_DOWN, hsend.at[0], hxrecv.at[1])
    feat_up.start()
    feat_down.start()

    def planes(i, carry):
        at = pl.ds(pl.multiple_of(i * 16, 16), 16)
        columns = xcol[at, :]
        v = [columns[:, d : d + 1] - xt[0, d : d + 1, :] for d in range(3)]
        unit, inv_r, basis, slopes = geometry(*v, weight[at, :], True)
        for k in range(NB):
            geo[k, at, :] = basis[k]
            geo[NB + k, at, :] = slopes[k]
        for d in range(3):
            geo[2 * NB + d, at, :] = unit[d]
        geo[2 * NB + 3, at, :] = inv_r
        ang = harmonics(*unit)
        for m in range(NM):
            for k in range(NB):
                product = basis[k] if m == 0 else basis[k] * ang[m]
                col = (m * NB + k) * ATOMS
                smat[at, col : col + ATOMS] = product.astype(BF16)
        return carry

    lax.fori_loop(0, 14, planes, 0)
    feat_up.wait()
    feat_down.wait()
    lane_c = lax.broadcasted_iota(jnp.int32, (C, ATOMS), 1)
    ht[1] = jnp.where(lane_c < 64, hxrecv[0].astype(F32), hxrecv[1].astype(F32)).astype(BF16)
    near = jnp.concatenate([ht[0], ht[1]], axis=1)
    picked = nn(near, ohy[...]).astype(BF16)
    hsend[1] = picked[:, :ATOMS]
    hsend[2] = picked[:, ATOMS:]
    feat_up = copy(FEAT, Y_UP, hsend.at[1], ht.at[2])
    feat_down = copy(FEAT, Y_DOWN, hsend.at[2], ht.at[3])
    feat_up.start()
    feat_down.start()
    lax.fori_loop(14, 27, planes, 0)
    feat_up.wait()
    feat_down.wait()
    near = jnp.concatenate([ht[b] for b in range(4)], axis=1)
    hsend[3] = nn(near, ohz[...]).astype(BF16)
    feat_z = copy(FEAT, Z_SWAP, hsend.at[3], ht.at[4])
    feat_z.start()
    lax.fori_loop(27, 40, planes, 0)
    feat_z.wait()

    whole = jnp.concatenate([ht[b] for b in range(5)], axis=1)
    for m in range(NM):
        part = nn(whole, smat[:, m * NB * ATOMS : (m + 1) * NB * ATOMS])
        total = None
        for k in range(NB):
            term = r2b[k] * part[:, k * ATOMS : (k + 1) * ATOMS]
            total = term if k == 0 else total + term
        amp2[m] = total
    inv[0:C, :] = amp2[0].astype(BF16)
    inv[C : 2 * C, :] = squares([amp2[m] for m in range(1, 4)]).astype(BF16)
    inv[2 * C :, :] = squares([amp2[m] for m in range(4, 9)]).astype(BF16)
    own = ht[0].astype(F32)
    h2 = nn(mixt2[...], inv[...]) + own
    pre = tn(rh[...], h2, precision=HIGHEST)
    sig = 1.0 / (1.0 + jnp.exp(-pre))
    filled = occ[0, 0].astype(F32)
    energy = nn(ro1[...], own, precision=HIGHEST) + nn(ro2[...], pre * sig, precision=HIGHEST)
    e_out[0, 0] = filled * energy
    dpre = tn(ro2[...], filled, precision=HIGHEST) * (sig * (1.0 + pre * (1.0 - sig)))
    dh2 = nn(rh[...], dpre, precision=HIGHEST)
    dinv = nn(mix2[...], dh2.astype(BF16))
    for m in range(NM):
        if m == 0:
            g = dinv[0:C]
        elif m < 4:
            g = 2.0 * dinv[C : 2 * C] * amp2[m]
        else:
            g = 2.0 * dinv[2 * C :] * amp2[m]
        for k in range(NB):
            col = (m * NB + k) * ATOMS
            ut[:, col : col + ATOMS] = (r2b[k] * g).astype(BF16)

    dh[4 * ATOMS :, :] = nt(smat[4 * ATOMS :, :], ut[...])
    gsend[4 * ATOMS :, :] = dh[4 * ATOMS :, :].astype(BF16)
    grad_z = copy(GRAD, Z_SWAP, gsend.at[pl.ds(4 * ATOMS, ATOMS), :], gzr)
    grad_z.start()
    dh[0 : 4 * ATOMS, :] = nt(smat[0 : 4 * ATOMS, :], ut[...])
    dh[0:ATOMS, :] += (dh2 + embb[1] * filled).T
    for b in range(5):
        hn[b * ATOMS : (b + 1) * ATOMS, :] = ht[b].astype(F32).T.astype(BF16)
    grad_z.wait()
    dh[0 : 4 * ATOMS, :] += nn(ohz[...], gzr[...])
    gsend[2 * ATOMS : 4 * ATOMS, :] = dh[2 * ATOMS : 4 * ATOMS, :].astype(BF16)
    grad_up = copy(GRAD, Y_UP, gsend.at[pl.ds(3 * ATOMS, ATOMS), :], gyr.at[pl.ds(ATOMS, ATOMS), :])
    grad_down = copy(GRAD, Y_DOWN, gsend.at[pl.ds(2 * ATOMS, ATOMS), :], gyr.at[pl.ds(0, ATOMS), :])
    grad_up.start()
    grad_down.start()

    def load_geo(at):
        return (
            [geo[2 * NB + d, at, :] for d in range(3)],
            geo[2 * NB + 3, at, :],
            [geo[k, at, :] for k in range(NB)],
            [geo[NB + k, at, :] for k in range(NB)],
        )

    def pull_two(b):
        for m in range(NM):
            cols = slice(m * NB * ATOMS, (m + 1) * NB * ATOMS)
            gam[:, cols] = nn(hn[b * ATOMS : (b + 1) * ATOMS, :], ut[:, cols])

        def body(i, carry):
            from_row = pl.ds(pl.multiple_of(i * 8, 8), 8)
            at = pl.ds(pl.multiple_of(b * ATOMS + i * 8, 8), 8)

            def gamma(m, k):
                col = (m * NB + k) * ATOMS
                return gam[from_row, col : col + ATOMS]

            out = edge_pull(gamma, *load_geo(at))
            for d in range(3):
                dv[d, at, :] = out[d]
            return carry

        lax.fori_loop(0, ATOMS // 8, body, 0)

    pull_two(0)
    pull_two(1)
    grad_up.wait()
    grad_down.wait()
    dh[0 : 2 * ATOMS, :] += nn(ohy[...], gyr[...])
    gsend[ATOMS : 2 * ATOMS, :] = dh[ATOMS : 2 * ATOMS, :].astype(BF16)
    half = ATOMS // 2
    grad_up = copy(GRAD, X_UP, gsend.at[pl.ds(ATOMS + half, half), :], gxr.at[pl.ds(half, half), :])
    grad_down = copy(GRAD, X_DOWN, gsend.at[pl.ds(ATOMS, half), :], gxr.at[pl.ds(0, half), :])
    grad_up.start()
    grad_down.start()
    pull_two(2)
    pull_two(3)
    pull_two(4)
    grad_up.wait()
    grad_down.wait()
    dh1 = dh[0:ATOMS, :] + nn(ohx[...], gxr[...])

    dinv = nt(mix1[...], dh1.astype(BF16))
    for m in range(NM):
        if m == 0:
            g = dinv[0:C]
        elif m < 4:
            g = 2.0 * dinv[C : 2 * C] * amp[m]
        else:
            g = 2.0 * dinv[2 * C :] * amp[m]
        moments = SPREAD * nn(r1[...], g, precision=HIGHEST)
        for k in range(NB):
            dm[m * NB + k] = jnp.broadcast_to(moments[k : k + 1, :], (8, ATOMS))

    def pull_one(i, totals):
        at = pl.ds(pl.multiple_of(i * 8, 8), 8)
        out = edge_pull(lambda m, k: dm[m * NB + k], *load_geo(at))
        result = []
        for d in range(3):
            both = out[d] + dv[d, at, :]
            dv[d, at, :] = both
            result.append(totals[d] + both)
        return tuple(result)

    zero = jnp.zeros((8, ATOMS), F32)
    totals = lax.fori_loop(0, EXT // 8, pull_one, (zero, zero, zero))
    ones = jnp.ones((8, ATOMS), F32)
    for d in range(3):
        column = nt(ones, dv[d], precision=HIGHEST)
        frow[d : d + 1, :] = column[0:1, :]
        frow[d : d + 1, 0:ATOMS] = column[0:1, 0:ATOMS] - jnp.sum(totals[d], axis=0, keepdims=True)

    def pack(slot, values):
        fsend[slot] = jnp.zeros((16, ATOMS), BF16)
        for i, part in enumerate(split3(values)):
            fsend[slot, 4 * i : 4 * i + 3, :] = part

    def spread(received, matrix):
        wide = nt(received, matrix)
        return wide[0:3, :] + wide[4:7, :] + wide[8:11, :]

    pack(0, frow[0:3, 4 * ATOMS :])
    force_z = copy(FORCE, Z_SWAP, fsend.at[0], frecv.at[0])
    force_z.start()
    force_z.wait()
    frow[0:3, 0 : 4 * ATOMS] += spread(frecv[0], ohz[...])
    pack(1, frow[0:3, 3 * ATOMS : 4 * ATOMS])
    pack(2, frow[0:3, 2 * ATOMS : 3 * ATOMS])
    force_up = copy(FORCE, Y_UP, fsend.at[1], frecv.at[1])
    force_down = copy(FORCE, Y_DOWN, fsend.at[2], frecv.at[2])
    force_up.start()
    force_down.start()
    force_up.wait()
    force_down.wait()
    frow[0:3, 0 : 2 * ATOMS] += spread(frecv[2], ohy[:, 0:ATOMS]) + spread(frecv[1], ohy[:, ATOMS:])
    pack(3, frow[0:3, ATOMS : 2 * ATOMS])
    force_up = copy(FORCE, X_UP, fsend.at[3], frecv.at[3])
    force_down = copy(FORCE, X_DOWN, fsend.at[3], frecv.at[4])
    force_up.start()
    force_down.start()
    force_up.wait()
    force_down.wait()
    lane_f = lax.broadcasted_iota(jnp.int32, (16, ATOMS), 1)
    merged = jnp.where(lane_f < 64, frecv[4].astype(F32), frecv[3].astype(F32)).astype(BF16)
    total = frow[0:3, 0:ATOMS] + spread(merged, ohx[...])
    for d in range(3):
        f_out[d, 0, 0] = -total[d : d + 1, :]


def per_device(
    positions, occupancy, neighbours, keep, face_x, face_y, face_z, radial_one, mix_one, embed,
    radial_two, mix_two, read_one, read_hidden, read_out,
):
    vmem = pl.BlockSpec(memory_space=pltpu.VMEM)
    cols = NB * NM * ATOMS
    scratch = [
        pltpu.VMEM((5, 8, ATOMS), F32),
        pltpu.VMEM((9, 8, ATOMS), F32),
        pltpu.VMEM((EXT, 8), F32),
        pltpu.VMEM((NEIGH, ATOMS), jnp.int32),
        pltpu.VMEM((NEIGH, ATOMS), jnp.int32),
        pltpu.VMEM((EXT, ATOMS), F32),
        pltpu.VMEM((ATOMS, ATOMS), BF16),
        pltpu.VMEM((2 * ATOMS, 2 * ATOMS), BF16),
        pltpu.VMEM((4 * ATOMS, ATOMS), BF16),
        pltpu.VMEM((NB, C, ATOMS), F32),
        pltpu.VMEM((NB, C, ATOMS), F32),
        pltpu.VMEM((C, 3 * C), BF16),
        pltpu.VMEM((C, 3 * C), BF16),
        pltpu.VMEM((2, C, ATOMS), F32),
        pltpu.VMEM((NM, C, ATOMS), F32),
        pltpu.VMEM((NM, C, ATOMS), F32),
        pltpu.VMEM((3 * C, ATOMS), BF16),
        pltpu.VMEM((5, C, ATOMS), BF16),
        pltpu.VMEM((EXT, C), BF16),
        pltpu.VMEM((4, C, ATOMS), BF16),
        pltpu.VMEM((2, C, ATOMS), BF16),
        pltpu.VMEM((EXT, cols), BF16),
        pltpu.VMEM((2 * NB + 4, EXT, ATOMS), F32),
        pltpu.VMEM((C, cols), BF16),
        pltpu.VMEM((ATOMS, cols), F32),
        pltpu.VMEM((3, EXT, ATOMS), F32),
        pltpu.VMEM((EXT, C), F32),
        pltpu.VMEM((EXT, C), BF16),
        pltpu.VMEM((ATOMS, C), BF16),
        pltpu.VMEM((2 * ATOMS, C), BF16),
        pltpu.VMEM((ATOMS, C), BF16),
        pltpu.VMEM((8, EXT), F32),
        pltpu.VMEM((4, 16, ATOMS), BF16),
        pltpu.VMEM((5, 16, ATOMS), BF16),
        pltpu.VMEM((NB * NM, 8, ATOMS), F32),
        pltpu.SemaphoreType.DMA((20,)),
        pltpu.SemaphoreType.DMA((20,)),
    ]
    return pl.pallas_call(
        kernel,
        out_shape=(
            jax.ShapeDtypeStruct(occupancy.shape, F32),
            jax.ShapeDtypeStruct(positions.shape, F32),
        ),
        in_specs=[vmem] * 15,
        out_specs=(vmem, vmem),
        scratch_shapes=scratch,
        compiler_params=pltpu.CompilerParams(
            collective_id=0, has_side_effects=True, vmem_limit_bytes=56 * 1024 * 1024
        ),
    )(
        positions, occupancy, neighbours, keep, face_x, face_y, face_z, radial_one, mix_one,
        embed.reshape(1, -1), radial_two, mix_two, read_one.reshape(1, -1), read_hidden,
        read_out.reshape(1, -1),
    )


def solution(mesh):
    return jax.shard_map(
        per_device,
        mesh=mesh,
        in_specs=(
            P(None, "gx", "gy", "gz", None),
            P("gx", "gy", "gz", None),
            P(None, "gx", "gy", "gz", None),
            P(None, "gx", "gy", "gz", None),
            P("gx", "gy", "gz", None, None),
            P("gx", "gy", "gz", None, None),
            P("gx", "gy", "gz", None),
            P(),
            P(),
            P(),
            P(),
            P(),
            P(),
            P(),
            P(),
        ),
        out_specs=(P("gx", "gy", "gz", None), P(None, "gx", "gy", "gz", None)),
        check_vma=False,
    )
```

profile of v0, /device:TPU:1, one launch (start us, length us, event | category | flops | bytes accessed | tf_op | source)
XLA Modules:
  0.0 69.7 jit_solution(5729595545563648707)
XLA Ops:
  0.6 1.4 %copy.17.rh = f32[128,16]{1,0:T(8,128)} copy(f32[128,16]{0,1:T(8,128)} %param.28) | data formatting | bytes 16384 | tf_op args[13]
  2.0 66.0 %shard_map.158 = (f32[1,1,1,128]{3,2,1,0:T(1,128)}, f32[3,1,1,1,128]{4,3,2,1,0:T(1,128)}) custom-call(f32[3,1,1,1,128]{4,3,2,1,0:T(1,128)} %pos.1, s32[1,1,1,128]{3,2,1,0:T(1,128)} %occ.1, s32[56,1,1,1,128]{4,3,2,1,0:T(1,128)} %nbr.1, s32[56,1,1,1,128]{4,3,2,1,0:T(1,128)} %keep.1, s32[1,1,1,2,64]{4,3,2,1,0:T(2,128)} %fx.1, s32[1,1,1,2,128]{4,3,2,1,0:T(2,128)} %fy.1, ...), custom_call_target="tpu_custom_call" | custom-call | tf_op jit(solution)/shard_map/pallas_call | solution.py:539
  68.0 0.0 copy-start.1
  68.1 0.0 copy-start
  68.1 0.6 copy-done.1
  68.6 0.5 copy.20
  69.2 0.0 copy-done
  69.2 0.6 copy.21
Async XLA Ops:
  68.0 0.6 copy-start.1
  68.1 1.1 %copy-start = (f32[3,1,1,1,128]{4,3,2,1,0:T(1,128)S(1)}, f32[3,1,1,1,128]{4,3,2,1,0:T(1,128)}, u32[]{:S(2)}) copy-start(f32[3,1,1,1,128]{4,3,2,1,0:T(1,128)} %get-tuple-element.5) | copy-start | bytes 4612
where the time goes:
time: 69.9 us; the launch traced here: 69.7 us
  Pallas kernels  66 us (94%)
  local copies, waits for them, and re-layouts  3.07 us (4%)
    pallas_call x1, Pallas kernels, per_device(): pl.pallas_call(kernel, out_shape=(jax.ShapeDtypeStruct(occupancy.shape, F...  66 us
    unnamed x7, local copies, waits for them, and re-layouts  3.07 us

commit v1 on v0

v1 whole, which is shorter than its diff:
```python
import functools
import math

import jax
import jax.numpy as jnp
from jax import lax
from jax.experimental import pallas as pl
from jax.experimental.pallas import tpu as pltpu
from jax.sharding import PartitionSpec as P

F32 = jnp.float32
BF16 = jnp.bfloat16
NB = 8
NM = 9
ATOMS = 128
NEIGH = 56
EXT = 640
C = 128
STEP_XY = 4 * 1.8
STEP_Z = 8 * 1.8
CUTOFF = 5.0
SPREAD = 0.4
HIGHEST = lax.Precision.HIGHEST
R3 = 3.0**0.5
R5 = 5.0**0.5
R15 = 15.0**0.5
MESH = pl.DeviceIdType.MESH

GROUPS = [(0, 0), (-1, 0), (1, 0), (0, 1), (-1, 1), (1, 1)]
NEAR = [(dx, dy, dz) for dz in (0, 1) for dy in (0, -1, 1) for dx in (-1, 1)]
NEAR += [(0, dy, dz) for dy, dz in GROUPS[:0:-1]]
POS, FEAT, GRAD, FORCE = 0, 1, 2, 3
GROUP = 2 * 128


def nn(a, b, **kw):
    return jnp.dot(a, b, preferred_element_type=F32, **kw)


def nt(a, b, **kw):
    return lax.dot_general(a, b, (((1,), (1,)), ((), ())), preferred_element_type=F32, **kw)


def tn(a, b, **kw):
    return lax.dot_general(a, b, (((0,), (0,)), ((), ())), preferred_element_type=F32, **kw)


def poly(x, coefficients):
    total = coefficients[-1]
    for c in coefficients[-2::-1]:
        total = total * x + c
    return total


COS_C = [(-1.0) ** i * math.pi ** (2 * i) / math.factorial(2 * i) for i in range(8)]
SIN_C = [(-1.0) ** i * math.pi ** (2 * i + 1) / math.factorial(2 * i + 1) for i in range(7)]


def geometry(vx, vy, vz, w, derivative):
    sq = jnp.where(w > 0.0, vx * vx + vy * vy + vz * vz, 1.0)
    inv_r = lax.rsqrt(sq)
    r = sq * inv_r
    ux, uy, uz = vx * inv_r, vy * inv_r, vz * inv_r
    s = jnp.minimum(r * (1.0 / CUTOFF), 1.0)
    t = 1.0 - s * s
    x = s - 0.5
    x2 = x * x
    sin1 = poly(x2, COS_C)
    cos1 = -x * poly(x2, SIN_C)
    p = w * ((2.0 / CUTOFF) ** 0.5 * inv_r)
    pt = p * t
    q = pt * t
    twice = 2.0 * cos1
    sins = [sin1, twice * sin1]
    for k in range(2, NB):
        sins.append(twice * sins[-1] - sins[-2])
    basis = [q * v for v in sins]
    if not derivative:
        return (ux, uy, uz), inv_r, basis, None
    coss = [cos1, twice * cos1 - 1.0]
    for k in range(2, NB):
        coss.append(twice * coss[-1] - coss[-2])
    q5 = q * (math.pi / CUTOFF)
    low = q * inv_r + pt * (s * (4.0 / CUTOFF))
    slopes = [(k + 1.0) * q5 * coss[k] - low * sins[k] for k in range(NB)]
    return (ux, uy, uz), inv_r, basis, slopes


def harmonics(ux, uy, uz):
    return [
        None,
        R3 * ux,
        R3 * uy,
        R3 * uz,
        R15 * ux * uy,
        R15 * uy * uz,
        0.5 * R5 * (3.0 * uz * uz - 1.0),
        R15 * ux * uz,
        0.5 * R15 * (ux * ux - uy * uy),
    ]


def edge_pull(gamma, unit, inv_r, basis, slopes):
    ux, uy, uz = unit
    ang = harmonics(ux, uy, uz)
    q = [gamma(0, k) for k in range(NB)]
    p = [None] * NM
    for m in range(1, NM):
        for k in range(NB):
            value = gamma(m, k)
            q[k] = q[k] + value * ang[m]
            term = value * basis[k]
            p[m] = term if k == 0 else p[m] + term
    radial = q[0] * slopes[0]
    for k in range(1, NB):
        radial = radial + q[k] * slopes[k]
    gx = R3 * p[1] + R15 * (uy * p[4] + uz * p[7] + ux * p[8])
    gy = R3 * p[2] + R15 * (ux * p[4] + uz * p[5] - uy * p[8])
    gz = R3 * p[3] + R15 * (uy * p[5] + ux * p[7]) + (3.0 * R5) * uz * p[6]
    along = radial - (gx * ux + gy * uy + gz * uz) * inv_r
    return gx * inv_r + along * ux, gy * inv_r + along * uy, gz * inv_r + along * uz


def squares(parts):
    total = parts[0] * parts[0]
    for part in parts[1:]:
        total = total + part * part
    return total


def split(x, parts):
    out = []
    for _ in range(parts):
        part = x.astype(BF16)
        out.append(part)
        x = x - part.astype(F32)
    return out


def equal(a, b):
    return jnp.where(a == b, 1.0, 0.0).astype(BF16)


def flip(offset):
    dx, dy, dz = offset
    return (-dx, -dy, dz)


def kernel(
    pos, occ, nbr, keep, fx, fy, fz, r1, mix1, emb, r2, mix2, ro1, rht, ro2,
    e_out, f_out,
    xt, psend, precv, xcol, nbrs, key, weight, hot, ohx, ohxt, oh, oht,
    r1b, r2b, mixt1, mixt2, embb, amp, amp2, inv, ht, hn, hx, hrecv, smat, geo, near, ut,
    gam, dv, dh, gsend, grecv, frow, fsend, frecv, dm, dvl, flat,
    send, recv,
):
    cx, cy, cz = lax.axis_index("gx"), lax.axis_index("gy"), lax.axis_index("gz")
    nx, ny, nz = lax.axis_size("gx"), lax.axis_size("gy"), lax.axis_size("gz")

    def device(offset):
        dx, dy, dz = offset
        return (lax.rem(cx + dx + nx, nx), lax.rem(cy + dy + ny, ny), lax.rem(cz + dz, nz))

    def copy(phase, offset, src, dst):
        i = NEAR.index(offset)
        j = NEAR.index(flip(offset))
        return pltpu.make_async_remote_copy(
            src_ref=src, dst_ref=dst, send_sem=send.at[phase, i], recv_sem=recv.at[phase, j],
            device_id=device(offset), device_id_type=MESH,
        )

    def exchange(phase, source, target):
        copies = [copy(phase, o, source(o), target(o)) for o in NEAR]
        for c in copies:
            c.start()
        return copies

    def finish(copies):
        for c in copies:
            c.wait_recv()
        for c in copies:
            c.wait_send()

    def rows_of(offset, along):
        dx, dy, dz = offset
        base = GROUPS.index((dy, dz)) * GROUP
        if along == 0:
            return pl.ds(base, ATOMS)
        return pl.ds(base + ATOMS + (0 if along < 0 else ATOMS // 2), ATOMS // 2)

    barrier = pltpu.get_barrier_semaphore()
    for offset in NEAR:
        pl.semaphore_signal(barrier, inc=1, device_id=device(offset), device_id_type=MESH)

    row = lax.broadcasted_iota(jnp.int32, (8, ATOMS), 0)
    lane = lax.broadcasted_iota(jnp.int32, (8, ATOMS), 1)

    def pick(ids, tiles):
        low = ids & (ATOMS - 1)
        total = jnp.take_along_axis(tiles[0], low, axis=1)
        for b in range(1, len(tiles)):
            here = jnp.take_along_axis(tiles[b], low, axis=1)
            total = jnp.where(ids >= b * ATOMS, here, total)
        return total

    psend[...] = jnp.zeros((2, 8, ATOMS), F32)
    for d in range(3):
        psend[0, d : d + 1, :] = pos[d, 0, 0]
    psend[0, 3:4, :] = fy[0, 0, 0, 1:2, :].astype(F32)
    psend[0, 4:5, :] = fy[0, 0, 0, 0:1, :].astype(F32)
    psend[0, 5:6, :] = fz[0, 0].astype(F32)
    xt[0] = psend[0]
    pick_x = jnp.concatenate([fx[0, 0, 0, 1:2, :], fx[0, 0, 0, 0:1, :]], axis=1)
    psend[1] = pick(jnp.broadcast_to(pick_x, (8, ATOMS)), [xt[0]])
    pl.semaphore_wait(barrier, len(NEAR))
    copies = exchange(
        POS,
        lambda o: psend.at[1 if o[0] else 0],
        lambda o: precv.at[NEAR.index(flip(o))],
    )

    for j in range(NEIGH):
        kept = keep[j, 0, 0]
        slot = nbr[j, 0, 0]
        key[j : j + 1, :] = jnp.where(kept > 0, slot, -1)
        nbrs[j : j + 1, :] = slot

    def weight_block(i, carry):
        base = pl.multiple_of(i * 32, 32)
        ids = [row + base + 8 * t for t in range(4)]
        total = [jnp.zeros((8, ATOMS), F32) for t in range(4)]
        for j in range(NEIGH):
            one = jnp.broadcast_to(key[j : j + 1, :], (8, ATOMS))
            found = [jnp.where(ids[t] == one, 1.0, 0.0) for t in range(4)]
            hot[pl.ds(base, 32), j * ATOMS : (j + 1) * ATOMS] = jnp.concatenate(found, axis=0).astype(BF16)
            for t in range(4):
                total[t] = total[t] + found[t]
        for t in range(4):
            weight[pl.ds(base + 8 * t, 8), :] = total[t]
        return carry

    lax.fori_loop(0, EXT // 32, weight_block, 0)
    square = (ATOMS, ATOMS)
    sub = lax.broadcasted_iota(jnp.int32, square, 0)
    along = lax.broadcasted_iota(jnp.int32, square, 1)
    ohx[...] = equal(sub, jnp.broadcast_to(pick_x, square))
    ohxt[...] = equal(along.astype(F32), jnp.broadcast_to(pick_x, square).astype(F32).T)
    for k in range(NB):
        r1b[k] = SPREAD * jnp.broadcast_to(r1[k : k + 1, :], (C, ATOMS)).T
        r2b[k] = SPREAD * jnp.broadcast_to(r2[k : k + 1, :], (C, ATOMS)).T
    for b in range(3):
        rows = slice(b * C, (b + 1) * C)
        mixt1[:, rows] = mix1[rows, :].astype(F32).T.astype(BF16)
        mixt2[:, rows] = mix2[rows, :].astype(F32).T.astype(BF16)
    embb[0] = jnp.broadcast_to(emb[...], (C, ATOMS)).T
    embb[1] = jnp.broadcast_to(ro1[...], (C, ATOMS)).T
    finish(copies)

    def received(dx, dy, dz):
        return precv[NEAR.index((dx, dy, dz))]

    def column(dy, dz):
        own = xt[0] if (dy, dz) == (0, 0) else received(0, dy, dz)
        side = jnp.where(lane < ATOMS // 2, received(-1, dy, dz), received(1, dy, dz))
        step = jnp.where(lane < ATOMS // 2, -STEP_XY, STEP_XY)
        side = side + jnp.where(row == 0, step, 0.0)
        shift = jnp.where(row == 1, dy * STEP_XY, 0.0)
        return [own, side] if dy == 0 else [own + shift, side + shift]

    def listed(dy, dz):
        source = received(0, dy, dz)
        at = 3 if dy < 0 else 4
        return jnp.broadcast_to(source[at : at + 1, :], (8, ATOMS)).astype(jnp.int32)

    own, side = column(0, 0)
    xt[1] = side
    low_y, high_y = listed(-1, 0), listed(1, 0)
    xt[2] = pick(low_y, column(-1, 0))
    xt[3] = pick(high_y, column(1, 0))
    other = jnp.broadcast_to(received(0, 0, 1)[5:6, :], (8, ATOMS)).astype(jnp.int32)
    low_bits = other & (ATOMS - 1)
    through_low = jnp.take_along_axis(listed(-1, 1), low_bits, axis=1)
    through_high = jnp.take_along_axis(listed(1, 1), low_bits, axis=1)
    far = jnp.where(other < 2 * ATOMS, other, through_low + 2 * ATOMS)
    far = jnp.where(other < 3 * ATOMS, far, through_high + 4 * ATOMS)
    upward = jnp.where(cz == 0, STEP_Z, -STEP_Z)
    xt[4] = pick(far, column(0, 1) + column(-1, 1) + column(1, 1)) + jnp.where(row == 2, upward, 0.0)

    slots = nbrs[...]
    kept = jnp.where(key[...] >= 0, 1.0, 0.0)
    offsets = []
    for d in range(3):
        tables = [jnp.broadcast_to(xt[b, d : d + 1, :], (8, ATOMS)) for b in range(5)]
        offsets.append(
            jnp.concatenate(
                [pick(slots[8 * i : 8 * i + 8, :], tables) - tables[0] for i in range(NEIGH // 8)],
                axis=0,
            )
        )
    unit, inv_r, basis, slopes = geometry(*offsets, kept, True)
    for k in range(NB):
        near[k] = basis[k]
        near[NB + k] = slopes[k]
    for d in range(3):
        near[2 * NB + d] = unit[d]
    near[2 * NB + 3] = inv_r
    ang = harmonics(*unit)
    for m in range(NM):
        total = None
        for k in range(NB):
            product = basis[k] if m == 0 else basis[k] * ang[m]
            moment = jnp.sum(product, axis=0, keepdims=True)
            term = r1b[k] * moment
            total = term if k == 0 else total + term
        amp[m] = total
    inv[0:C, :] = amp[0].astype(BF16)
    inv[C : 2 * C, :] = squares([amp[m] for m in range(1, 4)]).astype(BF16)
    inv[2 * C :, :] = squares([amp[m] for m in range(4, 9)]).astype(BF16)
    ht[0] = (nn(mixt1[...], inv[...]) + embb[0]).astype(BF16)
    hrecv[0:ATOMS, :] = ht[0].astype(F32).T.astype(BF16)
    hx[...] = nn(ohxt[...], hrecv[0:ATOMS, :]).astype(BF16)
    half = ATOMS // 2

    def feature_source(o):
        if o[0] == 0:
            return hrecv.at[pl.ds(0, ATOMS), :]
        return hx.at[pl.ds(0 if o[0] > 0 else half, half), :]

    copies = exchange(FEAT, feature_source, lambda o: hrecv.at[rows_of(flip(o), -o[0]), :])

    for b in range(5):
        xcol[b * ATOMS : (b + 1) * ATOMS, :] = xt[b].T
    column_ids = [
        jnp.broadcast_to(ids[0:1, :], square).astype(F32).T for ids in (low_y, high_y, far)
    ]
    row_ids = [jnp.broadcast_to(ids[0:1, :], square) for ids in (low_y, high_y, far)]
    at = 0
    for ids, ids_t, blocks in zip(row_ids, column_ids, (2, 2, 6)):
        for b in range(blocks):
            cut = slice(at * ATOMS, (at + 1) * ATOMS)
            oht[cut, :] = equal(sub + b * ATOMS, ids)
            oh[:, cut] = equal((along + b * ATOMS).astype(F32), ids_t)
            at = at + 1

    def planes(i, carry):
        at = pl.ds(pl.multiple_of(i * 16, 16), 16)
        columns = xcol[at, :]
        v = [columns[:, d : d + 1] - xt[0, d : d + 1, :] for d in range(3)]
        unit, inv_r, basis, slopes = geometry(*v, weight[at, :], True)
        for k in range(NB):
            geo[k, at, :] = basis[k]
            geo[NB + k, at, :] = slopes[k]
        for d in range(3):
            geo[2 * NB + d, at, :] = unit[d]
        geo[2 * NB + 3, at, :] = inv_r
        ang = harmonics(*unit)
        for m in range(NM):
            for k in range(NB):
                product = basis[k] if m == 0 else basis[k] * ang[m]
                col = (m * NB + k) * ATOMS
                smat[at, col : col + ATOMS] = product.astype(BF16)
        return carry

    lax.fori_loop(0, EXT // 16, planes, 0)
    finish(copies)
    hn[0:GROUP, :] = hrecv[0:GROUP, :]
    for b, first, blocks in ((2, 0, 2), (3, 2, 2), (4, 4, 6)):
        cut = slice(first * ATOMS, (first + blocks) * ATOMS)
        source = hrecv[GROUP + first * ATOMS : GROUP + (first + blocks) * ATOMS, :]
        hn[b * ATOMS : (b + 1) * ATOMS, :] = nn(oh[:, cut], source).astype(BF16)
    for b in range(1, 5):
        ht[b] = hn[b * ATOMS : (b + 1) * ATOMS, :].astype(F32).T.astype(BF16)

    whole = jnp.concatenate([ht[b] for b in range(5)], axis=1)
    for m in range(NM):
        part = nn(whole, smat[:, m * NB * ATOMS : (m + 1) * NB * ATOMS])
        total = None
        for k in range(NB):
            term = r2b[k] * part[:, k * ATOMS : (k + 1) * ATOMS]
            total = term if k == 0 else total + term
        amp2[m] = total
    inv[0:C, :] = amp2[0].astype(BF16)
    inv[C : 2 * C, :] = squares([amp2[m] for m in range(1, 4)]).astype(BF16)
    inv[2 * C :, :] = squares([amp2[m] for m in range(4, 9)]).astype(BF16)
    own = ht[0].astype(F32)
    h2 = nn(mixt2[...], inv[...]) + own
    pre = nn(rht[...], h2, precision=HIGHEST)
    sig = 1.0 / (1.0 + jnp.exp(-pre))
    filled = occ[0, 0].astype(F32)
    energy = nn(ro1[...], own, precision=HIGHEST) + nn(ro2[...], pre * sig, precision=HIGHEST)
    e_out[0, 0] = filled * energy
    dpre = tn(ro2[...], filled, precision=HIGHEST) * (sig * (1.0 + pre * (1.0 - sig)))
    dh2 = tn(rht[...], dpre, precision=HIGHEST)
    dinv = nn(mix2[...], dh2.astype(BF16))
    for m in range(NM):
        if m == 0:
            g = dinv[0:C]
        elif m < 4:
            g = 2.0 * dinv[C : 2 * C] * amp2[m]
        else:
            g = 2.0 * dinv[2 * C :] * amp2[m]
        for k in range(NB):
            col = (m * NB + k) * ATOMS
            ut[:, col : col + ATOMS] = (r2b[k] * g).astype(BF16)

    ghosts = nt(smat[ATOMS:, :], ut[...]).astype(BF16)
    gsend[ATOMS:GROUP, :] = ghosts[0:ATOMS, :]
    for b, first, blocks in ((1, 0, 2), (2, 2, 2), (3, 4, 6)):
        cut = slice(first * ATOMS, (first + blocks) * ATOMS)
        rows = slice(GROUP + first * ATOMS, GROUP + (first + blocks) * ATOMS)
        gsend[rows, :] = nn(oht[cut, :], ghosts[b * ATOMS : (b + 1) * ATOMS, :]).astype(BF16)
    copies = exchange(
        GRAD,
        lambda o: gsend.at[rows_of(o, o[0]), :],
        lambda o: grecv.at[rows_of(flip(o), o[0]), :],
    )
    dh[...] = nt(smat[0:ATOMS, :], ut[...]) + (dh2 + embb[1] * filled).T

    def load(planes, at):
        return (
            [planes[2 * NB + d, at, :] for d in range(3)],
            planes[2 * NB + 3, at, :],
            [planes[k, at, :] for k in range(NB)],
            [planes[NB + k, at, :] for k in range(NB)],
        )

    zero = jnp.zeros((8, ATOMS), F32)
    totals = (zero, zero, zero)
    for b in range(5):
        for m in range(NM):
            cols = slice(m * NB * ATOMS, (m + 1) * NB * ATOMS)
            gam[:, cols] = nn(hn[b * ATOMS : (b + 1) * ATOMS, :], ut[:, cols])

        def pull_two(i, totals):
            here = pl.ds(pl.multiple_of(i * 8, 8), 8)
            at = pl.ds(pl.multiple_of(b * ATOMS + i * 8, 8), 8)

            def gamma(m, k):
                col = (m * NB + k) * ATOMS
                return gam[here, col : col + ATOMS]

            out = edge_pull(gamma, *load(geo, at))
            for d in range(3):
                dv[d, at, :] = out[d]
            return tuple(totals[d] + out[d] for d in range(3))

        totals = lax.fori_loop(0, ATOMS // 8, pull_two, totals)
    ones = jnp.ones((8, ATOMS), F32)
    for d in range(3):
        line = nt(ones, dv[d], precision=HIGHEST)
        frow[d : d + 1, :] = line[0:1, :]
        frow[d : d + 1, 0:ATOMS] = line[0:1, 0:ATOMS] - jnp.sum(totals[d], axis=0, keepdims=True)
    finish(copies)
    slot_sum = dh[...]
    for g in range(1, 6):
        slot_sum = slot_sum + grecv[g * GROUP : g * GROUP + ATOMS, :].astype(F32)
    pick_sum = grecv[ATOMS:GROUP, :].astype(F32)
    for g in range(1, 6):
        pick_sum = pick_sum + grecv[g * GROUP + ATOMS : (g + 1) * GROUP, :].astype(F32)
    hi, low = split(pick_sum, 2)
    dh1 = slot_sum + nn(ohx[...], hi) + nn(ohx[...], low)

    dinv = nt(mix1[...], dh1.astype(BF16))
    for m in range(NM):
        if m == 0:
            g = dinv[0:C]
        elif m < 4:
            g = 2.0 * dinv[C : 2 * C] * amp[m]
        else:
            g = 2.0 * dinv[2 * C :] * amp[m]
        moments = SPREAD * nn(r1[...], g, precision=HIGHEST)
        for k in range(NB):
            dm[m * NB + k] = jnp.broadcast_to(moments[k : k + 1, :], (8, ATOMS))

    def pull_one(i, carry):
        at = pl.ds(pl.multiple_of(i * 8, 8), 8)
        out = edge_pull(lambda m, k: dm[m * NB + k], *load(near, at))
        for d in range(3):
            for part, value in enumerate(split(out[d], 2)):
                dvl[2 * d + part, at, :] = value.astype(F32)
        return carry

    lax.fori_loop(0, NEIGH // 8, pull_one, 0)
    flat[6:8, :] = jnp.zeros((2, NEIGH * ATOMS), F32)
    for n in range(6):
        for j in range(NEIGH):
            flat[n : n + 1, j * ATOMS : (j + 1) * ATOMS] = dvl[n, j : j + 1, :]
    lines = nt(flat[...].astype(BF16), hot[...])
    for d in range(3):
        frow[d : d + 1, :] += lines[2 * d : 2 * d + 1, :] + lines[2 * d + 1 : 2 * d + 2, :]
        frow[d : d + 1, 0:ATOMS] -= jnp.sum(dvl[2 * d] + dvl[2 * d + 1], axis=0, keepdims=True)

    def thrice(values):
        pad = jnp.zeros((1, values.shape[1]), F32)
        parts = [jnp.concatenate([p.astype(F32), pad], axis=0) for p in split(values, 3)]
        return jnp.concatenate(parts + [jnp.zeros((4, values.shape[1]), F32)], axis=0).astype(BF16)

    def merged(wide):
        return wide[0:3, :] + wide[4:7, :] + wide[8:11, :]

    fsend[...] = jnp.zeros(fsend.shape, F32)
    fsend[0, 0:3, :] = frow[0:3, ATOMS:GROUP]
    at = 0
    for b, blocks in ((2, 2), (3, 2), (4, 6)):
        cut = slice(at * ATOMS, (at + blocks) * ATOMS)
        values = merged(nn(thrice(frow[0:3, b * ATOMS : (b + 1) * ATOMS]), oh[:, cut]))
        for n in range(blocks):
            fsend[1 + at + n, 0:3, :] = values[:, n * ATOMS : (n + 1) * ATOMS]
        at = at + blocks

    def force_source(o):
        g = GROUPS.index((o[1], o[2]))
        return fsend.at[2 * g - 1 + (1 if o[0] else 0)]

    copies = exchange(FORCE, force_source, lambda o: frecv.at[NEAR.index(flip(o))])
    finish(copies)
    slot_sum = frow[0:3, 0:ATOMS]
    from_low = from_high = None
    for dy, dz in GROUPS:
        if (dy, dz) != (0, 0):
            slot_sum = slot_sum + frecv[NEAR.index((0, dy, dz)), 0:3, :]
        up, down = (frecv[NEAR.index((dx, dy, dz)), 0:3, :] for dx in (1, -1))
        from_high = up if from_high is None else from_high + up
        from_low = down if from_low is None else from_low + down
    pick_sum = jnp.where(lane[0:3, :] < half, from_high, from_low)
    total = slot_sum + merged(nt(thrice(pick_sum), ohx[...]))
    for d in range(3):
        f_out[d, 0, 0] = -total[d : d + 1, :]


def per_device(
    positions, occupancy, neighbours, keep, face_x, face_y, face_z, radial_one, mix_one, embed,
    radial_two, mix_two, read_one, read_hidden, read_out,
):
    vmem = pl.BlockSpec(memory_space=pltpu.VMEM)
    cols = NB * NM * ATOMS
    scratch = [
        pltpu.VMEM((5, 8, ATOMS), F32),
        pltpu.VMEM((2, 8, ATOMS), F32),
        pltpu.VMEM((17, 8, ATOMS), F32),
        pltpu.VMEM((EXT, 8), F32),
        pltpu.VMEM((NEIGH, ATOMS), jnp.int32),
        pltpu.VMEM((NEIGH, ATOMS), jnp.int32),
        pltpu.VMEM((EXT, ATOMS), F32),
        pltpu.VMEM((EXT, NEIGH * ATOMS), BF16),
        pltpu.VMEM((ATOMS, ATOMS), BF16),
        pltpu.VMEM((ATOMS, ATOMS), BF16),
        pltpu.VMEM((ATOMS, 10 * ATOMS), BF16),
        pltpu.VMEM((10 * ATOMS, ATOMS), BF16),
        pltpu.VMEM((NB, C, ATOMS), F32),
        pltpu.VMEM((NB, C, ATOMS), F32),
        pltpu.VMEM((C, 3 * C), BF16),
        pltpu.VMEM((C, 3 * C), BF16),
        pltpu.VMEM((2, C, ATOMS), F32),
        pltpu.VMEM((NM, C, ATOMS), F32),
        pltpu.VMEM((NM, C, ATOMS), F32),
        pltpu.VMEM((3 * C, ATOMS), BF16),
        pltpu.VMEM((5, C, ATOMS), BF16),
        pltpu.VMEM((EXT, C), BF16),
        pltpu.VMEM((ATOMS, C), BF16),
        pltpu.VMEM((6 * GROUP, C), BF16),
        pltpu.VMEM((EXT, cols), BF16),
        pltpu.VMEM((2 * NB + 4, EXT, ATOMS), F32),
        pltpu.VMEM((2 * NB + 4, NEIGH, ATOMS), F32),
        pltpu.VMEM((C, cols), BF16),
        pltpu.VMEM((ATOMS, cols), F32),
        pltpu.VMEM((3, EXT, ATOMS), F32),
        pltpu.VMEM((ATOMS, C), F32),
        pltpu.VMEM((6 * GROUP, C), BF16),
        pltpu.VMEM((6 * GROUP, C), BF16),
        pltpu.VMEM((8, EXT), F32),
        pltpu.VMEM((11, 8, ATOMS), F32),
        pltpu.VMEM((17, 8, ATOMS), F32),
        pltpu.VMEM((NB * NM, 8, ATOMS), F32),
        pltpu.VMEM((6, NEIGH, ATOMS), F32),
        pltpu.VMEM((8, NEIGH * ATOMS), F32),
        pltpu.SemaphoreType.DMA((4, 17)),
        pltpu.SemaphoreType.DMA((4, 17)),
    ]
    return pl.pallas_call(
        kernel,
        out_shape=(
            jax.ShapeDtypeStruct(occupancy.shape, F32),
            jax.ShapeDtypeStruct(positions.shape, F32),
        ),
        in_specs=[vmem] * 15,
        out_specs=(vmem, vmem),
        scratch_shapes=scratch,
        compiler_params=pltpu.CompilerParams(
            collective_id=0, has_side_effects=True, vmem_limit_bytes=56 * 1024 * 1024
        ),
    )(
        positions, occupancy, neighbours, keep, face_x, face_y, face_z, radial_one, mix_one,
        embed.reshape(1, -1), radial_two, mix_two, read_one.reshape(1, -1), read_hidden.T,
        read_out.reshape(1, -1),
    )


def solution(mesh):
    return jax.shard_map(
        per_device,
        mesh=mesh,
        in_specs=(
            P(None, "gx", "gy", "gz", None),
            P("gx", "gy", "gz", None),
            P(None, "gx", "gy", "gz", None),
            P(None, "gx", "gy", "gz", None),
            P("gx", "gy", "gz", None, None),
            P("gx", "gy", "gz", None, None),
            P("gx", "gy", "gz", None),
            P(),
            P(),
            P(),
            P(),
            P(),
            P(),
            P(),
            P(),
        ),
        out_specs=(P("gx", "gy", "gz", None), P(None, "gx", "gy", "gz", None)),
        check_vma=False,
    )
```

time: 69.9 us -> 58.2 us (0.83)
  Pallas kernels: 66 us -> 55.7 us
  local copies, waits for them, and re-layouts: 3.07 us -> 1.69 us
    pallas_call x1, Pallas kernels: 66 us -> 55.7 us  [per_device(): pl.pallas_call(kernel, out_shape=(jax.ShapeDtypeStruct(occupancy.shape, F...]
    unnamed x7 -> x6, local copies, waits for them, and re-layouts: 3.07 us -> 1.69 us
where the time goes in v1:
time: 58.2 us; the launch traced here: 58 us
  Pallas kernels  55.7 us (96%)
  local copies, waits for them, and re-layouts  1.69 us (3%)
  between operations  0.66 us (1%)
    pallas_call x1, Pallas kernels, per_device(): pl.pallas_call(kernel, out_shape=(jax.ShapeDtypeStruct(occupancy.shape, F...  55.7 us
    unnamed x6, local copies, waits for them, and re-layouts  1.69 us

profile of v1, /device:TPU:1, one launch (start us, length us, event | category | flops | bytes accessed | tf_op | source)
XLA Modules:
  0.0 58.0 jit_solution(7690381215312013122)
XLA Ops:
  0.6 55.7 %shard_map.158 = (f32[1,1,1,128]{3,2,1,0:T(1,128)}, f32[3,1,1,1,128]{4,3,2,1,0:T(1,128)}) custom-call(f32[3,1,1,1,128]{4,3,2,1,0:T(1,128)} %pos.1, s32[1,1,1,128]{3,2,1,0:T(1,128)} %occ.1, s32[56,1,1,1,128]{4,3,2,1,0:T(1,128)} %nbr.1, s32[56,1,1,1,128]{4,3,2,1,0:T(1,128)} %keep.1, s32[1,1,1,2,64]{4,3,2,1,0:T(2,128)} %fx.1, s32[1,1,1,2,128]{4,3,2,1,0:T(2,128)} %fy.1, ...), custom_call_target="tpu_custom_call" | custom-call | tf_op jit(solution)/shard_map/pallas_call | solution.py:580
  56.3 0.0 copy-start.1
  56.3 0.0 copy-start
  56.3 0.6 %copy-done.1 = f32[1,1,1,128]{3,2,1,0:T(1,128)S(1)} copy-done((f32[1,1,1,128]{3,2,1,0:T(1,128)S(1)}, f32[1,1,1,128]{3,2,1,0:T(1,128)}, u32[]{:S(2)}) %copy-start.1) | copy-done | bytes 536
  56.9 0.5 copy.19
  57.4 0.0 copy-done
  57.5 0.6 copy.20
Async XLA Ops:
  56.3 0.6 %copy-start.1 = (f32[1,1,1,128]{3,2,1,0:T(1,128)S(1)}, f32[1,1,1,128]{3,2,1,0:T(1,128)}, u32[]{:S(2)}) copy-start(f32[1,1,1,128]{3,2,1,0:T(1,128)} %get-tuple-element.4) | copy-start | bytes 1540
  56.3 1.1 %copy-start = (f32[3,1,1,1,128]{4,3,2,1,0:T(1,128)S(1)}, f32[3,1,1,1,128]{4,3,2,1,0:T(1,128)}, u32[]{:S(2)}) copy-start(f32[3,1,1,1,128]{4,3,2,1,0:T(1,128)} %get-tuple-element.5) | copy-start | bytes 4612

commit v2 on v1

--- a/solution.py
+++ b/solution.py
@@ -31,6 +31,8 @@
 NEAR += [(0, dy, dz) for dy, dz in GROUPS[:0:-1]]
 POS, FEAT, GRAD, FORCE = 0, 1, 2, 3
 GROUP = 2 * 128
+TILE = 16
+PART = 320
 
 
 def nn(a, b, **kw):
@@ -104,19 +106,29 @@
     ux, uy, uz = unit
     ang = harmonics(ux, uy, uz)
     q = [gamma(0, k) for k in range(NB)]
-    p = [None] * NM
-    for m in range(1, NM):
+
+    def radial_sum(m):
+        total = None
         for k in range(NB):
             value = gamma(m, k)
             q[k] = q[k] + value * ang[m]
             term = value * basis[k]
-            p[m] = term if k == 0 else p[m] + term
+            total = term if total is None else total + term
+        return total
+
+    gx, gy, gz = (R3 * radial_sum(m) for m in (1, 2, 3))
+    p = R15 * radial_sum(4)
+    gx, gy = gx + uy * p, gy + ux * p
+    p = R15 * radial_sum(5)
+    gy, gz = gy + uz * p, gz + uy * p
+    gz = gz + (3.0 * R5) * uz * radial_sum(6)
+    p = R15 * radial_sum(7)
+    gx, gz = gx + uz * p, gz + ux * p
+    p = R15 * radial_sum(8)
+    gx, gy = gx + ux * p, gy - uy * p
     radial = q[0] * slopes[0]
     for k in range(1, NB):
         radial = radial + q[k] * slopes[k]
-    gx = R3 * p[1] + R15 * (uy * p[4] + uz * p[7] + ux * p[8])
-    gy = R3 * p[2] + R15 * (ux * p[4] + uz * p[5] - uy * p[8])
-    gz = R3 * p[3] + R15 * (uy * p[5] + ux * p[7]) + (3.0 * R5) * uz * p[6]
     along = radial - (gx * ux + gy * uy + gz * uz) * inv_r
     return gx * inv_r + along * ux, gy * inv_r + along * uy, gz * inv_r + along * uz
 
@@ -141,19 +153,35 @@
     return jnp.where(a == b, 1.0, 0.0).astype(BF16)
 
 
+def over(count, step, body):
+    if step == count:
+        body(0, step)
+        return
+
+    def run(i, carry):
+        body(i, step)
+        return carry
+
+    lax.fori_loop(0, count // step, run, 0)
+
+
 def flip(offset):
     dx, dy, dz = offset
     return (-dx, -dy, dz)
 
 
 def kernel(
-    pos, occ, nbr, keep, fx, fy, fz, r1, mix1, emb, r2, mix2, ro1, rht, ro2,
-    e_out, f_out,
-    xt, psend, precv, xcol, nbrs, key, weight, hot, ohx, ohxt, oh, oht,
-    r1b, r2b, mixt1, mixt2, embb, amp, amp2, inv, ht, hn, hx, hrecv, smat, geo, near, ut,
-    gam, dv, dh, gsend, grecv, frow, fsend, frecv, dm, dvl, flat,
-    send, recv,
+    *refs,
 ):
+    given, (e_out, f_out) = refs[:15], refs[15:17]
+    held, loaded = refs[17:32], refs[32]
+    pos, occ, nbr, keep, fx, fy, fz, r1, mix1, emb, r2, mix2, ro1, rht, ro2 = held
+    (
+        xt, psend, precv, xcol, nbrs, key, local, weight, hot, ohx, ohxt, oh, oht,
+        r1b, r2b, mixt1, mixt2, embb, moments, amp, amp2, pulls, inv, ht, hn, hx, hrecv, smat, geo, near, ut, un, dghost,
+        gam, dv, dh, gsend, grecv, frow, fcol, pulled, fsend, frecv, dm, dvl, flat, turned,
+        send, recv,
+    ) = refs[33:]
     cx, cy, cz = lax.axis_index("gx"), lax.axis_index("gy"), lax.axis_index("gz")
     nx, ny, nz = lax.axis_size("gx"), lax.axis_size("gy"), lax.axis_size("gz")
 
@@ -191,6 +219,14 @@
     barrier = pltpu.get_barrier_semaphore()
     for offset in NEAR:
         pl.semaphore_signal(barrier, inc=1, device_id=device(offset), device_id_type=MESH)
+    loads = [
+        pltpu.make_async_copy(given[n], held[n], loaded.at[n]) for n in range(len(held))
+    ]
+    order = [0, 4, 5, 6, 2, 3, 7, 10, 8, 11, 9, 12, 1, 13, 14]
+    for n in order:
+        loads[n].start()
+    for n in order[:4]:
+        loads[n].wait()
 
     row = lax.broadcasted_iota(jnp.int32, (8, ATOMS), 0)
     lane = lax.broadcasted_iota(jnp.int32, (8, ATOMS), 1)
@@ -212,6 +248,34 @@
     xt[0] = psend[0]
     pick_x = jnp.concatenate([fx[0, 0, 0, 1:2, :], fx[0, 0, 0, 0:1, :]], axis=1)
     psend[1] = pick(jnp.broadcast_to(pick_x, (8, ATOMS)), [xt[0]])
+    for n in order[4:6]:
+        loads[n].wait()
+    def list_row(j, carry):
+        slot = nbr[j, 0, 0]
+        nbrs[pl.ds(j, 1), :] = slot
+        value = jnp.where(keep[j, 0, 0] > 0, slot, -1)
+        key[pl.ds(j, 1), :] = value
+        for b in range(5):
+            inside = (value >= b * ATOMS) & (value < (b + 1) * ATOMS)
+            inside = jnp.where(inside, value - b * ATOMS, -1).astype(F32)
+            local[b, j] = jnp.broadcast_to(inside, (16, ATOMS)).astype(BF16)
+        return carry
+
+    lax.fori_loop(0, NEIGH, list_row, 0, unroll=2)
+    for n in order[6:]:
+        loads[n].wait()
+    def spread_row(k, carry):
+        r1b[k] = SPREAD * jnp.broadcast_to(r1[pl.ds(k, 1), :], (C, ATOMS)).T
+        r2b[k] = SPREAD * jnp.broadcast_to(r2[pl.ds(k, 1), :], (C, ATOMS)).T
+        return carry
+
+    lax.fori_loop(0, NB, spread_row, 0)
+    for b in range(3):
+        rows = slice(b * C, (b + 1) * C)
+        mixt1[:, rows] = mix1[rows, :].astype(F32).T.astype(BF16)
+        mixt2[:, rows] = mix2[rows, :].astype(F32).T.astype(BF16)
+    embb[0] = jnp.broadcast_to(emb[...], (C, ATOMS)).T
+    embb[1] = jnp.broadcast_to(ro1[...], (C, ATOMS)).T
     pl.semaphore_wait(barrier, len(NEAR))
     copies = exchange(
         POS,
@@ -219,24 +283,30 @@
         lambda o: precv.at[NEAR.index(flip(o))],
     )
 
-    for j in range(NEIGH):
-        kept = keep[j, 0, 0]
-        slot = nbr[j, 0, 0]
-        key[j : j + 1, :] = jnp.where(kept > 0, slot, -1)
-        nbrs[j : j + 1, :] = slot
-
-    def weight_block(i, carry):
-        base = pl.multiple_of(i * 32, 32)
-        ids = [row + base + 8 * t for t in range(4)]
-        total = [jnp.zeros((8, ATOMS), F32) for t in range(4)]
-        for j in range(NEIGH):
-            one = jnp.broadcast_to(key[j : j + 1, :], (8, ATOMS))
-            found = [jnp.where(ids[t] == one, 1.0, 0.0) for t in range(4)]
-            hot[pl.ds(base, 32), j * ATOMS : (j + 1) * ATOMS] = jnp.concatenate(found, axis=0).astype(BF16)
-            for t in range(4):
-                total[t] = total[t] + found[t]
-        for t in range(4):
-            weight[pl.ds(base + 8 * t, 8), :] = total[t]
+    row16 = lax.broadcasted_iota(jnp.int32, (16, ATOMS), 0).astype(F32)
+    one16 = jnp.ones((16, ATOMS), BF16)
+    nil16 = jnp.zeros((16, ATOMS), BF16)
+
+    def weight_block(n, carry):
+        b = n // 4
+        i = n % 4
+        ids = [(row16 + (i * 32 + 16 * t).astype(F32)).astype(BF16) for t in range(2)]
+        at = [pl.ds(pl.multiple_of(n * 32 + 16 * t, 16), 16) for t in range(2)]
+
+        def scan(j8, total):
+            total = list(total)
+            for jj in range(8):
+                one = local[b, j8 * 8 + jj]
+                to = pl.ds(pl.multiple_of((j8 * 8 + jj) * ATOMS, ATOMS), ATOMS)
+                for t in range(2):
+                    found = jnp.where(ids[t] == one, one16, nil16)
+                    hot[at[t], to] = found
+                    total[t] = total[t] + found
+            return tuple(total)
+
+        total = lax.fori_loop(0, NEIGH // 8, scan, (nil16, nil16))
+        for t in range(2):
+            weight[at[t], :] = total[t].astype(F32)
         return carry
 
     lax.fori_loop(0, EXT // 32, weight_block, 0)
@@ -245,15 +315,6 @@
     along = lax.broadcasted_iota(jnp.int32, square, 1)
     ohx[...] = equal(sub, jnp.broadcast_to(pick_x, square))
     ohxt[...] = equal(along.astype(F32), jnp.broadcast_to(pick_x, square).astype(F32).T)
-    for k in range(NB):
-        r1b[k] = SPREAD * jnp.broadcast_to(r1[k : k + 1, :], (C, ATOMS)).T
-        r2b[k] = SPREAD * jnp.broadcast_to(r2[k : k + 1, :], (C, ATOMS)).T
-    for b in range(3):
-        rows = slice(b * C, (b + 1) * C)
-        mixt1[:, rows] = mix1[rows, :].astype(F32).T.astype(BF16)
-        mixt2[:, rows] = mix2[rows, :].astype(F32).T.astype(BF16)
-    embb[0] = jnp.broadcast_to(emb[...], (C, ATOMS)).T
-    embb[1] = jnp.broadcast_to(ro1[...], (C, ATOMS)).T
     finish(copies)
 
     def received(dx, dy, dz):
@@ -286,38 +347,45 @@
     upward = jnp.where(cz == 0, STEP_Z, -STEP_Z)
     xt[4] = pick(far, column(0, 1) + column(-1, 1) + column(1, 1)) + jnp.where(row == 2, upward, 0.0)
 
-    slots = nbrs[...]
-    kept = jnp.where(key[...] >= 0, 1.0, 0.0)
-    offsets = []
-    for d in range(3):
-        tables = [jnp.broadcast_to(xt[b, d : d + 1, :], (8, ATOMS)) for b in range(5)]
-        offsets.append(
-            jnp.concatenate(
-                [pick(slots[8 * i : 8 * i + 8, :], tables) - tables[0] for i in range(NEIGH // 8)],
-                axis=0,
-            )
-        )
-    unit, inv_r, basis, slopes = geometry(*offsets, kept, True)
-    for k in range(NB):
-        near[k] = basis[k]
-        near[NB + k] = slopes[k]
-    for d in range(3):
-        near[2 * NB + d] = unit[d]
-    near[2 * NB + 3] = inv_r
-    ang = harmonics(*unit)
-    for m in range(NM):
+    moments[...] = jnp.zeros(moments.shape, F32)
+
+    def list_tile(i, carry):
+        at = pl.ds(pl.multiple_of(i * 8, 8), 8)
+        ids = nbrs[at, :]
+        kept = jnp.where(key[at, :] >= 0, 1.0, 0.0)
+        offset = []
+        for d in range(3):
+            tables = [jnp.broadcast_to(xt[b, d : d + 1, :], (8, ATOMS)) for b in range(5)]
+            offset.append(pick(ids, tables) - tables[0])
+        unit, inv_r, basis, slopes = geometry(*offset, kept, True)
+        for k in range(NB):
+            near[k, at, :] = basis[k]
+            near[NB + k, at, :] = slopes[k]
+        for d in range(3):
+            near[2 * NB + d, at, :] = unit[d]
+        near[2 * NB + 3, at, :] = inv_r
+        ang = harmonics(*unit)
+        for m in range(NM):
+            for k in range(NB):
+                moments[m * NB + k] += basis[k] if m == 0 else basis[k] * ang[m]
+        return carry
+
+    lax.fori_loop(0, NEIGH // 8, list_tile, 0)
+
+    def first_amplitude(m, carry):
         total = None
         for k in range(NB):
-            product = basis[k] if m == 0 else basis[k] * ang[m]
-            moment = jnp.sum(product, axis=0, keepdims=True)
-            term = r1b[k] * moment
+            term = r1b[k] * jnp.sum(moments[m * NB + k], axis=0, keepdims=True)
             total = term if k == 0 else total + term
         amp[m] = total
+        return carry
+
+    lax.fori_loop(0, NM, first_amplitude, 0)
     inv[0:C, :] = amp[0].astype(BF16)
     inv[C : 2 * C, :] = squares([amp[m] for m in range(1, 4)]).astype(BF16)
     inv[2 * C :, :] = squares([amp[m] for m in range(4, 9)]).astype(BF16)
     ht[0] = (nn(mixt1[...], inv[...]) + embb[0]).astype(BF16)
-    hrecv[0:ATOMS, :] = ht[0].astype(F32).T.astype(BF16)
+    hrecv[0:ATOMS, :] = ht[0].T
     hx[...] = nn(ohxt[...], hrecv[0:ATOMS, :]).astype(BF16)
     half = ATOMS // 2
 
@@ -362,6 +430,25 @@
         return carry
 
     lax.fori_loop(0, EXT // 16, planes, 0)
+    def chunk(m, step=1):
+        width = NB * ATOMS * step
+        if isinstance(m, int):
+            return pl.ds(m * width, width)
+        return pl.ds(pl.multiple_of(m * width, width), width)
+
+    def amplitude(m, source, rows):
+        part = nn(source, smat[rows, chunk(m)])
+        total = None
+        for k in range(NB):
+            term = r2b[k] * part[:, k * ATOMS : (k + 1) * ATOMS]
+            total = term if k == 0 else total + term
+        return total
+
+    def amplitude_own(i, step):
+        for t in range(step):
+            amp2[i * step + t] = amplitude(i * step + t, ht[0], slice(0, ATOMS))
+
+    over(NM, 3, amplitude_own)
     finish(copies)
     hn[0:GROUP, :] = hrecv[0:GROUP, :]
     for b, first, blocks in ((2, 0, 2), (3, 2, 2), (4, 4, 6)):
@@ -369,16 +456,14 @@
         source = hrecv[GROUP + first * ATOMS : GROUP + (first + blocks) * ATOMS, :]
         hn[b * ATOMS : (b + 1) * ATOMS, :] = nn(oh[:, cut], source).astype(BF16)
     for b in range(1, 5):
-        ht[b] = hn[b * ATOMS : (b + 1) * ATOMS, :].astype(F32).T.astype(BF16)
-
-    whole = jnp.concatenate([ht[b] for b in range(5)], axis=1)
-    for m in range(NM):
-        part = nn(whole, smat[:, m * NB * ATOMS : (m + 1) * NB * ATOMS])
-        total = None
-        for k in range(NB):
-            term = r2b[k] * part[:, k * ATOMS : (k + 1) * ATOMS]
-            total = term if k == 0 else total + term
-        amp2[m] = total
+        ht[b] = hn[b * ATOMS : (b + 1) * ATOMS, :].T
+
+    whole = jnp.concatenate([ht[b] for b in range(1, 5)], axis=1)
+    def amplitude_ghosts(i, step):
+        for t in range(step):
+            amp2[i * step + t] += amplitude(i * step + t, whole, slice(ATOMS, EXT))
+
+    over(NM, 9, amplitude_ghosts)
     inv[0:C, :] = amp2[0].astype(BF16)
     inv[C : 2 * C, :] = squares([amp2[m] for m in range(1, 4)]).astype(BF16)
     inv[2 * C :, :] = squares([amp2[m] for m in range(4, 9)]).astype(BF16)
@@ -392,18 +477,34 @@
     dpre = tn(ro2[...], filled, precision=HIGHEST) * (sig * (1.0 + pre * (1.0 - sig)))
     dh2 = tn(rht[...], dpre, precision=HIGHEST)
     dinv = nn(mix2[...], dh2.astype(BF16))
-    for m in range(NM):
-        if m == 0:
-            g = dinv[0:C]
-        elif m < 4:
-            g = 2.0 * dinv[C : 2 * C] * amp2[m]
+    pulls[...] = dinv
+
+    def pulled_amplitude(m, values):
+        square = jnp.where(m < 4, pulls[C : 2 * C, :], pulls[2 * C :, :])
+        return jnp.where(m == 0, pulls[0:C, :], 2.0 * square * values[m])
+
+    def rows_two(m, carry):
+        g = pulled_amplitude(m, amp2)
+        turned = SPREAD * g.T
+        for k in range(NB):
+            at = pl.ds(pl.multiple_of((m * NB + k) * ATOMS, ATOMS), ATOMS)
+            ut[:, at] = (r2b[k] * g).astype(BF16)
+            un[at, :] = (turned * r2[k : k + 1, :]).astype(BF16)
+        return carry
+
+    lax.fori_loop(0, NM, rows_two, 0)
+
+    def ghost_part(i, step):
+        part = nn(smat[ATOMS:, chunk(i, step)], un[chunk(i, step), :])
+        if step == NM:
+            dghost[...] = part
         else:
-            g = 2.0 * dinv[2 * C :] * amp2[m]
-        for k in range(NB):
-            col = (m * NB + k) * ATOMS
-            ut[:, col : col + ATOMS] = (r2b[k] * g).astype(BF16)
-
-    ghosts = nt(smat[ATOMS:, :], ut[...]).astype(BF16)
+            dghost[...] += part
+
+    if 9 < NM:
+        dghost[...] = jnp.zeros(dghost.shape, F32)
+    over(NM, 9, ghost_part)
+    ghosts = dghost[...].astype(BF16)
     gsend[ATOMS:GROUP, :] = ghosts[0:ATOMS, :]
     for b, first, blocks in ((1, 0, 2), (2, 2, 2), (3, 4, 6)):
         cut = slice(first * ATOMS, (first + blocks) * ATOMS)
@@ -414,7 +515,12 @@
         lambda o: gsend.at[rows_of(o, o[0]), :],
         lambda o: grecv.at[rows_of(flip(o), o[0]), :],
     )
-    dh[...] = nt(smat[0:ATOMS, :], ut[...]) + (dh2 + embb[1] * filled).T
+    dh[...] = (dh2 + embb[1] * filled).T
+
+    def own_part(i, step):
+        dh[...] += nn(smat[0:ATOMS, chunk(i, step)], un[chunk(i, step), :])
+
+    over(NM, 3, own_part)
 
     def load(planes, at):
         return (
@@ -424,16 +530,22 @@
             [planes[NB + k, at, :] for k in range(NB)],
         )
 
-    zero = jnp.zeros((8, ATOMS), F32)
+    zero = jnp.zeros((TILE, ATOMS), F32)
     totals = (zero, zero, zero)
-    for b in range(5):
-        for m in range(NM):
-            cols = slice(m * NB * ATOMS, (m + 1) * NB * ATOMS)
-            gam[:, cols] = nn(hn[b * ATOMS : (b + 1) * ATOMS, :], ut[:, cols])
+
+    def pull_part(b, totals):
+        base = pl.multiple_of(b * PART, PART)
+
+        def gammas(i, step):
+            for t in range(step):
+                at = chunk(i * step + t)
+                gam[:, at] = nn(hn[pl.ds(base, PART), :], ut[:, at])
+
+        over(NM, 9, gammas)
 
         def pull_two(i, totals):
-            here = pl.ds(pl.multiple_of(i * 8, 8), 8)
-            at = pl.ds(pl.multiple_of(b * ATOMS + i * 8, 8), 8)
+            here = pl.ds(pl.multiple_of(i * TILE, TILE), TILE)
+            at = pl.ds(pl.multiple_of(base + i * TILE, TILE), TILE)
 
             def gamma(m, k):
                 col = (m * NB + k) * ATOMS
@@ -444,12 +556,18 @@
                 dv[d, at, :] = out[d]
             return tuple(totals[d] + out[d] for d in range(3))
 
-        totals = lax.fori_loop(0, ATOMS // 8, pull_two, totals)
-    ones = jnp.ones((8, ATOMS), F32)
+        return lax.fori_loop(0, PART // TILE, pull_two, totals)
+
+    totals = lax.fori_loop(0, EXT // PART, pull_part, totals)
+    total = None
     for d in range(3):
-        line = nt(ones, dv[d], precision=HIGHEST)
-        frow[d : d + 1, :] = line[0:1, :]
-        frow[d : d + 1, 0:ATOMS] = line[0:1, 0:ATOMS] - jnp.sum(totals[d], axis=0, keepdims=True)
+        take = jnp.where(along == 2 * d, 1.0, 0.0).astype(BF16)
+        for part in split(dv[d], 2):
+            term = nn(part, take)
+            total = term if total is None else total + term
+    fcol[...] = total
+    for d in range(3):
+        pulled[d : d + 1, :] = jnp.sum(totals[d], axis=0, keepdims=True)
     finish(copies)
     slot_sum = dh[...]
     for g in range(1, 6):
@@ -461,16 +579,15 @@
     dh1 = slot_sum + nn(ohx[...], hi) + nn(ohx[...], low)
 
     dinv = nt(mix1[...], dh1.astype(BF16))
-    for m in range(NM):
-        if m == 0:
-            g = dinv[0:C]
-        elif m < 4:
-            g = 2.0 * dinv[C : 2 * C] * amp[m]
-        else:
-            g = 2.0 * dinv[2 * C :] * amp[m]
-        moments = SPREAD * nn(r1[...], g, precision=HIGHEST)
+    pulls[...] = dinv
+
+    def rows_one(m, carry):
+        lines = SPREAD * nn(r1[...], pulled_amplitude(m, amp), precision=HIGHEST)
         for k in range(NB):
-            dm[m * NB + k] = jnp.broadcast_to(moments[k : k + 1, :], (8, ATOMS))
+            dm[m * NB + k] = jnp.broadcast_to(lines[k : k + 1, :], (8, ATOMS))
+        return carry
+
+    lax.fori_loop(0, NM, rows_one, 0)
 
     def pull_one(i, carry):
         at = pl.ds(pl.multiple_of(i * 8, 8), 8)
@@ -482,13 +599,35 @@
 
     lax.fori_loop(0, NEIGH // 8, pull_one, 0)
     flat[6:8, :] = jnp.zeros((2, NEIGH * ATOMS), F32)
-    for n in range(6):
-        for j in range(NEIGH):
-            flat[n : n + 1, j * ATOMS : (j + 1) * ATOMS] = dvl[n, j : j + 1, :]
-    lines = nt(flat[...].astype(BF16), hot[...])
-    for d in range(3):
-        frow[d : d + 1, :] += lines[2 * d : 2 * d + 1, :] + lines[2 * d + 1 : 2 * d + 2, :]
-        frow[d : d + 1, 0:ATOMS] -= jnp.sum(dvl[2 * d] + dvl[2 * d + 1], axis=0, keepdims=True)
+
+    def flat_row(j, carry):
+        to = pl.ds(pl.multiple_of(j * ATOMS, ATOMS), ATOMS)
+        for n in range(6):
+            flat[n : n + 1, to] = dvl[n, pl.ds(j, 1), :]
+        return carry
+
+    lax.fori_loop(0, NEIGH, flat_row, 0, unroll=4)
+
+    def turn(n, carry):
+        at = pl.ds(pl.multiple_of(n * 8 * ATOMS, 8 * ATOMS), 8 * ATOMS)
+        turned[at, :] = flat[:, at].T.astype(BF16)
+        return carry
+
+    lax.fori_loop(0, NEIGH // 8, turn, 0)
+
+    def lines_of(first, last):
+        def part(i, step):
+            at = chunk(i, step)
+            fcol[first:last, 0:8] += nn(hot[first:last, at], turned[at, :])
+
+        over(NEIGH // 8, 7, part)
+        for b in range(first // ATOMS, last // ATOMS):
+            lines = fcol[b * ATOMS : (b + 1) * ATOMS, 0:8].T
+            for d in range(3):
+                line = lines[2 * d : 2 * d + 1, :] + lines[2 * d + 1 : 2 * d + 2, :]
+                frow[d : d + 1, b * ATOMS : (b + 1) * ATOMS] = line
+
+    lines_of(ATOMS, EXT)
 
     def thrice(values):
         pad = jnp.zeros((1, values.shape[1]), F32)
@@ -513,8 +652,11 @@
         return fsend.at[2 * g - 1 + (1 if o[0] else 0)]
 
     copies = exchange(FORCE, force_source, lambda o: frecv.at[NEAR.index(flip(o))])
+    lines_of(0, ATOMS)
+    for d in range(3):
+        pulled[d : d + 1, :] += jnp.sum(dvl[2 * d] + dvl[2 * d + 1], axis=0, keepdims=True)
     finish(copies)
-    slot_sum = frow[0:3, 0:ATOMS]
+    slot_sum = frow[0:3, 0:ATOMS] - pulled[0:3, :]
     from_low = from_high = None
     for dy, dz in GROUPS:
         if (dy, dz) != (0, 0):
@@ -534,13 +676,21 @@
 ):
     vmem = pl.BlockSpec(memory_space=pltpu.VMEM)
     cols = NB * NM * ATOMS
-    scratch = [
+    operands = (
+        positions, occupancy, neighbours, keep, face_x, face_y, face_z, radial_one, mix_one,
+        embed.reshape(1, -1), radial_two, mix_two, read_one.reshape(1, -1), read_hidden.T,
+        read_out.reshape(1, -1),
+    )
+    scratch = [pltpu.VMEM(v.shape, v.dtype) for v in operands]
+    scratch += [
+        pltpu.SemaphoreType.DMA((len(operands),)),
         pltpu.VMEM((5, 8, ATOMS), F32),
         pltpu.VMEM((2, 8, ATOMS), F32),
         pltpu.VMEM((17, 8, ATOMS), F32),
         pltpu.VMEM((EXT, 8), F32),
         pltpu.VMEM((NEIGH, ATOMS), jnp.int32),
         pltpu.VMEM((NEIGH, ATOMS), jnp.int32),
+        pltpu.VMEM((5, NEIGH, 16, ATOMS), BF16),
         pltpu.VMEM((EXT, ATOMS), F32),
         pltpu.VMEM((EXT, NEIGH * ATOMS), BF16),
         pltpu.VMEM((ATOMS, ATOMS), BF16),
@@ -552,8 +702,10 @@
         pltpu.VMEM((C, 3 * C), BF16),
         pltpu.VMEM((C, 3 * C), BF16),
         pltpu.VMEM((2, C, ATOMS), F32),
+        pltpu.VMEM((NB * NM, 8, ATOMS), F32),
         pltpu.VMEM((NM, C, ATOMS), F32),
         pltpu.VMEM((NM, C, ATOMS), F32),
+        pltpu.VMEM((3 * C, ATOMS), F32),
         pltpu.VMEM((3 * C, ATOMS), BF16),
         pltpu.VMEM((5, C, ATOMS), BF16),
         pltpu.VMEM((EXT, C), BF16),
@@ -563,17 +715,22 @@
         pltpu.VMEM((2 * NB + 4, EXT, ATOMS), F32),
         pltpu.VMEM((2 * NB + 4, NEIGH, ATOMS), F32),
         pltpu.VMEM((C, cols), BF16),
-        pltpu.VMEM((ATOMS, cols), F32),
+        pltpu.VMEM((cols, C), BF16),
+        pltpu.VMEM((4 * ATOMS, C), F32),
+        pltpu.VMEM((PART, cols), F32),
         pltpu.VMEM((3, EXT, ATOMS), F32),
         pltpu.VMEM((ATOMS, C), F32),
         pltpu.VMEM((6 * GROUP, C), BF16),
         pltpu.VMEM((6 * GROUP, C), BF16),
         pltpu.VMEM((8, EXT), F32),
+        pltpu.VMEM((EXT, ATOMS), F32),
+        pltpu.VMEM((8, ATOMS), F32),
         pltpu.VMEM((11, 8, ATOMS), F32),
         pltpu.VMEM((17, 8, ATOMS), F32),
         pltpu.VMEM((NB * NM, 8, ATOMS), F32),
         pltpu.VMEM((6, NEIGH, ATOMS), F32),
         pltpu.VMEM((8, NEIGH * ATOMS), F32),
+        pltpu.VMEM((NEIGH * ATOMS, 8), BF16),
         pltpu.SemaphoreType.DMA((4, 17)),
         pltpu.SemaphoreType.DMA((4, 17)),
     ]
@@ -583,17 +740,13 @@
             jax.ShapeDtypeStruct(occupancy.shape, F32),
             jax.ShapeDtypeStruct(positions.shape, F32),
         ),
-        in_specs=[vmem] * 15,
+        in_specs=[pl.BlockSpec(memory_space=pl.ANY)] * len(operands),
         out_specs=(vmem, vmem),
         scratch_shapes=scratch,
         compiler_params=pltpu.CompilerParams(
             collective_id=0, has_side_effects=True, vmem_limit_bytes=56 * 1024 * 1024
         ),
-    )(
-        positions, occupancy, neighbours, keep, face_x, face_y, face_z, radial_one, mix_one,
-        embed.reshape(1, -1), radial_two, mix_two, read_one.reshape(1, -1), read_hidden.T,
-        read_out.reshape(1, -1),
-    )
+    )(*operands)
 
 
 def solution(mesh):

time: 58.2 us -> 55.3 us (0.950)
  Pallas kernels: 55.7 us -> 52.7 us
    pallas_call x1, Pallas kernels: 55.7 us -> 52.7 us  [per_device(): pl.pallas_call(kernel, out_shape=(jax.ShapeDtypeStruct(occupancy.shape, F...]
where the time goes in v2:
time: 55.3 us; the launch traced here: 55 us
  Pallas kernels  52.7 us (95%)
  local copies, waits for them, and re-layouts  1.69 us (3%)
  between operations  0.66 us (1%)
    pallas_call x1, Pallas kernels, per_device(): pl.pallas_call(kernel, out_shape=(jax.ShapeDtypeStruct(occupancy.shape, F...  52.7 us
    unnamed x6, local copies, waits for them, and re-layouts  1.69 us

profile of v2, /device:TPU:1, one launch (start us, length us, event | category | flops | bytes accessed | tf_op | source)
XLA Modules:
  0.0 55.0 jit_solution(9369271583536037600)
XLA Ops:
  0.6 52.7 %shard_map.158 = (f32[1,1,1,128]{3,2,1,0:T(1,128)}, f32[3,1,1,1,128]{4,3,2,1,0:T(1,128)}) custom-call(f32[3,1,1,1,128]{4,3,2,1,0:T(1,128)} %refs_0_.1, s32[1,1,1,128]{3,2,1,0:T(1,128)} %refs_1_.1, s32[56,1,1,1,128]{4,3,2,1,0:T(1,128)} %refs_2_.1, s32[56,1,1,1,128]{4,3,2,1,0:T(1,128)} %refs_3_.1, s32[1,1,1,2,64]{4,3,2,1,0:T(2,128)} %refs_4_.1, ...), custom_call_target="tpu_custom_call" | custom-call | tf_op jit(solution)/shard_map/pallas_call | solution.py:737
  53.3 0.0 copy-start.1
  53.3 0.0 copy-start
  53.3 0.6 %copy-done.1 = f32[1,1,1,128]{3,2,1,0:T(1,128)S(1)} copy-done((f32[1,1,1,128]{3,2,1,0:T(1,128)S(1)}, f32[1,1,1,128]{3,2,1,0:T(1,128)}, u32[]{:S(2)}) %copy-start.1) | copy-done | bytes 536
  53.9 0.5 copy.19
  54.5 0.0 copy-done
  54.5 0.6 %copy.20 = f32[3,1,1,1,128]{4,3,2,1,0:T(1,128)} copy(f32[3,1,1,1,128]{4,3,2,1,0:T(1,128)S(1)} %copy-done) | data formatting | bytes 3072
Async XLA Ops:
  53.3 0.6 %copy-start.1 = (f32[1,1,1,128]{3,2,1,0:T(1,128)S(1)}, f32[1,1,1,128]{3,2,1,0:T(1,128)}, u32[]{:S(2)}) copy-start(f32[1,1,1,128]{3,2,1,0:T(1,128)} %get-tuple-element.4) | copy-start | bytes 1540
  53.3 1.1 %copy-start = (f32[3,1,1,1,128]{4,3,2,1,0:T(1,128)S(1)}, f32[3,1,1,1,128]{4,3,2,1,0:T(1,128)}, u32[]{:S(2)}) copy-start(f32[3,1,1,1,128]{4,3,2,1,0:T(1,128)} %get-tuple-element.5) | copy-start | bytes 4612

commit v3 on v2

--- a/solution.py
+++ b/solution.py
@@ -32,7 +32,8 @@
 POS, FEAT, GRAD, FORCE = 0, 1, 2, 3
 GROUP = 2 * 128
 TILE = 16
-PART = 320
+PART = 256
+ROWS = 16
 
 
 def nn(a, b, **kw):
@@ -179,7 +180,7 @@
     (
         xt, psend, precv, xcol, nbrs, key, local, weight, hot, ohx, ohxt, oh, oht,
         r1b, r2b, mixt1, mixt2, embb, moments, amp, amp2, pulls, inv, ht, hn, hx, hrecv, smat, geo, near, ut, un, dghost,
-        gam, dv, dh, gsend, grecv, frow, fcol, pulled, fsend, frecv, dm, dvl, flat, turned,
+        gam, dv, dh, gsend, grecv, frow, pulled, fsend, frecv, dm, dvl, flat,
         send, recv,
     ) = refs[33:]
     cx, cy, cz = lax.axis_index("gx"), lax.axis_index("gy"), lax.axis_index("gz")
@@ -372,15 +373,16 @@
 
     lax.fori_loop(0, NEIGH // 8, list_tile, 0)
 
-    def first_amplitude(m, carry):
-        total = None
-        for k in range(NB):
-            term = r1b[k] * jnp.sum(moments[m * NB + k], axis=0, keepdims=True)
-            total = term if k == 0 else total + term
-        amp[m] = total
-        return carry
-
-    lax.fori_loop(0, NM, first_amplitude, 0)
+    def first_amplitude(i, step):
+        for m in range(step):
+            m = i * step + m
+            total = None
+            for k in range(NB):
+                term = r1b[k] * jnp.sum(moments[m * NB + k], axis=0, keepdims=True)
+                total = term if k == 0 else total + term
+            amp[m] = total
+
+    over(NM, 3, first_amplitude)
     inv[0:C, :] = amp[0].astype(BF16)
     inv[C : 2 * C, :] = squares([amp[m] for m in range(1, 4)]).astype(BF16)
     inv[2 * C :, :] = squares([amp[m] for m in range(4, 9)]).astype(BF16)
@@ -411,7 +413,7 @@
             at = at + 1
 
     def planes(i, carry):
-        at = pl.ds(pl.multiple_of(i * 16, 16), 16)
+        at = pl.ds(pl.multiple_of(i * ROWS, ROWS), ROWS)
         columns = xcol[at, :]
         v = [columns[:, d : d + 1] - xt[0, d : d + 1, :] for d in range(3)]
         unit, inv_r, basis, slopes = geometry(*v, weight[at, :], True)
@@ -429,7 +431,7 @@
                 smat[at, col : col + ATOMS] = product.astype(BF16)
         return carry
 
-    lax.fori_loop(0, EXT // 16, planes, 0)
+    lax.fori_loop(0, EXT // ROWS, planes, 0, unroll=2)
     def chunk(m, step=1):
         width = NB * ATOMS * step
         if isinstance(m, int):
@@ -448,7 +450,7 @@
         for t in range(step):
             amp2[i * step + t] = amplitude(i * step + t, ht[0], slice(0, ATOMS))
 
-    over(NM, 3, amplitude_own)
+    over(NM, 9, amplitude_own)
     finish(copies)
     hn[0:GROUP, :] = hrecv[0:GROUP, :]
     for b, first, blocks in ((2, 0, 2), (3, 2, 2), (4, 4, 6)):
@@ -483,16 +485,17 @@
         square = jnp.where(m < 4, pulls[C : 2 * C, :], pulls[2 * C :, :])
         return jnp.where(m == 0, pulls[0:C, :], 2.0 * square * values[m])
 
-    def rows_two(m, carry):
-        g = pulled_amplitude(m, amp2)
-        turned = SPREAD * g.T
-        for k in range(NB):
-            at = pl.ds(pl.multiple_of((m * NB + k) * ATOMS, ATOMS), ATOMS)
-            ut[:, at] = (r2b[k] * g).astype(BF16)
-            un[at, :] = (turned * r2[k : k + 1, :]).astype(BF16)
-        return carry
-
-    lax.fori_loop(0, NM, rows_two, 0)
+    def rows_two(i, step):
+        for t in range(step):
+            m = i * step + t
+            g = pulled_amplitude(m, amp2)
+            turned = SPREAD * g.T
+            for k in range(NB):
+                at = pl.ds(pl.multiple_of((m * NB + k) * ATOMS, ATOMS), ATOMS)
+                ut[:, at] = (r2b[k] * g).astype(BF16)
+                un[at, :] = (turned * r2[k : k + 1, :]).astype(BF16)
+
+    over(NM, 9, rows_two)
 
     def ghost_part(i, step):
         part = nn(smat[ATOMS:, chunk(i, step)], un[chunk(i, step), :])
@@ -533,15 +536,13 @@
     zero = jnp.zeros((TILE, ATOMS), F32)
     totals = (zero, zero, zero)
 
-    def pull_part(b, totals):
-        base = pl.multiple_of(b * PART, PART)
-
+    def pull_part(base, count, step, totals):
         def gammas(i, step):
             for t in range(step):
                 at = chunk(i * step + t)
-                gam[:, at] = nn(hn[pl.ds(base, PART), :], ut[:, at])
-
-        over(NM, 9, gammas)
+                gam[0:count, at] = nn(hn[pl.ds(base, count), :], ut[:, at])
+
+        over(NM, step, gammas)
 
         def pull_two(i, totals):
             here = pl.ds(pl.multiple_of(i * TILE, TILE), TILE)
@@ -556,18 +557,28 @@
                 dv[d, at, :] = out[d]
             return tuple(totals[d] + out[d] for d in range(3))
 
-        return lax.fori_loop(0, PART // TILE, pull_two, totals)
-
-    totals = lax.fori_loop(0, EXT // PART, pull_part, totals)
-    total = None
-    for d in range(3):
-        take = jnp.where(along == 2 * d, 1.0, 0.0).astype(BF16)
-        for part in split(dv[d], 2):
-            term = nn(part, take)
-            total = term if total is None else total + term
-    fcol[...] = total
-    for d in range(3):
-        pulled[d : d + 1, :] = jnp.sum(totals[d], axis=0, keepdims=True)
+        return lax.fori_loop(0, count // TILE, pull_two, totals)
+
+    def ghost_pull(b, totals):
+        return pull_part(pl.multiple_of(ATOMS + b * PART, ATOMS), PART, NM, totals)
+
+    totals = lax.fori_loop(0, 4 * ATOMS // PART, ghost_pull, totals)
+
+    def lines_two(first, last):
+        rows = slice(first, last)
+        total = None
+        for d in range(3):
+            take = jnp.where(along == 2 * d, 1.0, 0.0).astype(BF16)
+            for part in split(dv[d, rows, :], 2):
+                term = nn(part, take)
+                total = term if total is None else total + term
+        for b in range((last - first) // ATOMS):
+            lines = total[b * ATOMS : (b + 1) * ATOMS, :].T
+            for d in range(3):
+                at = slice(first + b * ATOMS, first + (b + 1) * ATOMS)
+                frow[d : d + 1, at] = lines[2 * d : 2 * d + 1, :]
+
+    lines_two(ATOMS, EXT)
     finish(copies)
     slot_sum = dh[...]
     for g in range(1, 6):
@@ -581,13 +592,14 @@
     dinv = nt(mix1[...], dh1.astype(BF16))
     pulls[...] = dinv
 
-    def rows_one(m, carry):
-        lines = SPREAD * nn(r1[...], pulled_amplitude(m, amp), precision=HIGHEST)
-        for k in range(NB):
-            dm[m * NB + k] = jnp.broadcast_to(lines[k : k + 1, :], (8, ATOMS))
-        return carry
-
-    lax.fori_loop(0, NM, rows_one, 0)
+    def rows_one(i, step):
+        for t in range(step):
+            m = i * step + t
+            lines = SPREAD * nn(r1[...], pulled_amplitude(m, amp), precision=HIGHEST)
+            for k in range(NB):
+                dm[m * NB + k] = jnp.broadcast_to(lines[k : k + 1, :], (8, ATOMS))
+
+    over(NM, 3, rows_one)
 
     def pull_one(i, carry):
         at = pl.ds(pl.multiple_of(i * 8, 8), 8)
@@ -597,7 +609,7 @@
                 dvl[2 * d + part, at, :] = value.astype(F32)
         return carry
 
-    lax.fori_loop(0, NEIGH // 8, pull_one, 0)
+    lax.fori_loop(0, NEIGH // 8, pull_one, 0, unroll=7)
     flat[6:8, :] = jnp.zeros((2, NEIGH * ATOMS), F32)
 
     def flat_row(j, carry):
@@ -608,24 +620,12 @@
 
     lax.fori_loop(0, NEIGH, flat_row, 0, unroll=4)
 
-    def turn(n, carry):
-        at = pl.ds(pl.multiple_of(n * 8 * ATOMS, 8 * ATOMS), 8 * ATOMS)
-        turned[at, :] = flat[:, at].T.astype(BF16)
-        return carry
-
-    lax.fori_loop(0, NEIGH // 8, turn, 0)
+    packed = flat[...].astype(BF16)
 
     def lines_of(first, last):
-        def part(i, step):
-            at = chunk(i, step)
-            fcol[first:last, 0:8] += nn(hot[first:last, at], turned[at, :])
-
-        over(NEIGH // 8, 7, part)
-        for b in range(first // ATOMS, last // ATOMS):
-            lines = fcol[b * ATOMS : (b + 1) * ATOMS, 0:8].T
-            for d in range(3):
-                line = lines[2 * d : 2 * d + 1, :] + lines[2 * d + 1 : 2 * d + 2, :]
-                frow[d : d + 1, b * ATOMS : (b + 1) * ATOMS] = line
+        wide = nt(packed, hot[first:last, :])
+        for d in range(3):
+            frow[d : d + 1, first:last] += wide[2 * d : 2 * d + 1, :] + wide[2 * d + 1 : 2 * d + 2, :]
 
     lines_of(ATOMS, EXT)
 
@@ -652,6 +652,10 @@
         return fsend.at[2 * g - 1 + (1 if o[0] else 0)]
 
     copies = exchange(FORCE, force_source, lambda o: frecv.at[NEAR.index(flip(o))])
+    totals = pull_part(0, ATOMS, 3, totals)
+    lines_two(0, ATOMS)
+    for d in range(3):
+        pulled[d : d + 1, :] = jnp.sum(totals[d], axis=0, keepdims=True)
     lines_of(0, ATOMS)
     for d in range(3):
         pulled[d : d + 1, :] += jnp.sum(dvl[2 * d] + dvl[2 * d + 1], axis=0, keepdims=True)
@@ -723,14 +727,12 @@
         pltpu.VMEM((6 * GROUP, C), BF16),
         pltpu.VMEM((6 * GROUP, C), BF16),
         pltpu.VMEM((8, EXT), F32),
-        pltpu.VMEM((EXT, ATOMS), F32),
         pltpu.VMEM((8, ATOMS), F32),
         pltpu.VMEM((11, 8, ATOMS), F32),
         pltpu.VMEM((17, 8, ATOMS), F32),
         pltpu.VMEM((NB * NM, 8, ATOMS), F32),
         pltpu.VMEM((6, NEIGH, ATOMS), F32),
         pltpu.VMEM((8, NEIGH * ATOMS), F32),
-        pltpu.VMEM((NEIGH * ATOMS, 8), BF16),
         pltpu.SemaphoreType.DMA((4, 17)),
         pltpu.SemaphoreType.DMA((4, 17)),
     ]

time: 55.3 us -> 49.9 us (0.902)
  Pallas kernels: 52.7 us -> 47.4 us
    pallas_call x1, Pallas kernels: 52.7 us -> 47.4 us  [per_device(): pl.pallas_call(kernel, out_shape=(jax.ShapeDtypeStruct(occupancy.shape, F...]
where the time goes in v3:
time: 49.9 us; the launch traced here: 49.7 us
  Pallas kernels  47.4 us (95%)
  local copies, waits for them, and re-layouts  1.69 us (3%)
  between operations  0.66 us (1%)
    pallas_call x1, Pallas kernels, per_device(): pl.pallas_call(kernel, out_shape=(jax.ShapeDtypeStruct(occupancy.shape, F...  47.4 us
    unnamed x6, local copies, waits for them, and re-layouts  1.69 us

profile of v3, /device:TPU:1, one launch (start us, length us, event | category | flops | bytes accessed | tf_op | source)
XLA Modules:
  0.0 49.7 jit_solution(10557096372165380822)
XLA Ops:
  0.6 47.4 %shard_map.158 = (f32[1,1,1,128]{3,2,1,0:T(1,128)}, f32[3,1,1,1,128]{4,3,2,1,0:T(1,128)}) custom-call(f32[3,1,1,1,128]{4,3,2,1,0:T(1,128)} %refs_0_.1, s32[1,1,1,128]{3,2,1,0:T(1,128)} %refs_1_.1, s32[56,1,1,1,128]{4,3,2,1,0:T(1,128)} %refs_2_.1, s32[56,1,1,1,128]{4,3,2,1,0:T(1,128)} %refs_3_.1, s32[1,1,1,2,64]{4,3,2,1,0:T(2,128)} %refs_4_.1, ...), custom_call_target="tpu_custom_call" | custom-call | tf_op jit(solution)/shard_map/pallas_call | solution.py:739
  48.0 0.0 copy-start.1
  48.0 0.0 copy-start
  48.0 0.6 %copy-done.1 = f32[1,1,1,128]{3,2,1,0:T(1,128)S(1)} copy-done((f32[1,1,1,128]{3,2,1,0:T(1,128)S(1)}, f32[1,1,1,128]{3,2,1,0:T(1,128)}, u32[]{:S(2)}) %copy-start.1) | copy-done | bytes 536
  48.7 0.5 %copy.19 = f32[1,1,1,128]{3,2,1,0:T(1,128)} copy(f32[1,1,1,128]{3,2,1,0:T(1,128)S(1)} %copy-done.1) | data formatting | bytes 1024
  49.2 0.0 copy-done
  49.2 0.6 %copy.20 = f32[3,1,1,1,128]{4,3,2,1,0:T(1,128)} copy(f32[3,1,1,1,128]{4,3,2,1,0:T(1,128)S(1)} %copy-done) | data formatting | bytes 3072
Async XLA Ops:
  48.0 0.6 %copy-start.1 = (f32[1,1,1,128]{3,2,1,0:T(1,128)S(1)}, f32[1,1,1,128]{3,2,1,0:T(1,128)}, u32[]{:S(2)}) copy-start(f32[1,1,1,128]{3,2,1,0:T(1,128)} %get-tuple-element.4) | copy-start | bytes 1540
  48.0 1.1 %copy-start = (f32[3,1,1,1,128]{4,3,2,1,0:T(1,128)S(1)}, f32[3,1,1,1,128]{4,3,2,1,0:T(1,128)}, u32[]{:S(2)}) copy-start(f32[3,1,1,1,128]{4,3,2,1,0:T(1,128)} %get-tuple-element.5) | copy-start | bytes 4612
